TPU v7x, 256 devices: a whole 4x4x8 slice. The times are simulated.
256 devices in a mesh: rep: 8 (over z_lo, core), fsdp: 32 (over x, y, z_hi).
Axes of the slice: x: 4, y: 4, z: 8 (z_hi: 2, z_lo: 4; z = z_hi * 4 + z_lo), core: 2. Of those that a mesh axis runs over, the one named last changes fastest.
Arguments:
- inputs: bfloat16 [8, 12288, 8192], P('rep', 'fsdp'), may hold values from -12 to 12
- cotangent: bfloat16 [8, 12288, 512], P('rep', 'fsdp'), may hold values from -0.3125 to 0.3125
- weights: float32 [8, 8192, 512], P('rep', 'fsdp'), may hold values from -0.0625 to 0.0625
- first_moment: float32 [8, 8192, 512], P('rep', 'fsdp'), may hold values from -1.75 to 1.75
- second_moment: float32 [8, 8192, 512], P('rep', 'fsdp'), may hold values from 0.1 to 4
- pseudo_grad: float32 [8, 8192, 128], P('rep', 'fsdp'), may hold values from -6 to 6
- anchor: float32 [8192, 512], P('fsdp'), may hold values from -3 to 3
- momentum: float32 [8192, 512], P('fsdp'), may hold values from -6 to 6
- fragment: int32 [1], replicated, may hold values from 0 to 3
Outputs:
- projected: bfloat16 [8, 12288, 512], P('rep', 'fsdp')
- new_weights: float32 [8, 8192, 512], P('rep', 'fsdp')
- new_first: float32 [8, 8192, 512], P('rep', 'fsdp')
- new_second: float32 [8, 8192, 512], P('rep', 'fsdp')
- new_anchor: float32 [8192, 512], P('fsdp')
- new_momentum: float32 [8192, 512], P('fsdp')
All inputs are finite; a program needn't handle non-finite values.
Results may differ from a plain program's by a relative error of at most 0.0049.
Values may be sent and summed in bfloat16 or wider, within the bound.
A program may use at most 128 MiB of HBM per device.

v0:
```python
import jax
import jax.numpy as jnp
from jax import lax
from jax.sharding import PartitionSpec as P

beta_one = 0.9
beta_two = 0.95
inner_rate = 0.002
weight_decay = 0.1
adam_epsilon = 1e-08
outer_rate = 0.7
outer_momentum = 0.9


def shards(
    inputs, cotangent, weights, first_moment, second_moment, pseudo_grad, anchor, momentum, fragment
):
    tokens = inputs[0]
    grads_in = cotangent[0]
    master = weights[0]
    frag_w = pseudo_grad.shape[2]
    frag_start = fragment[0] * frag_w
    zero_index = jnp.zeros((), jnp.int32)
    groups = lax.axis_size("rep")
    summed = lax.psum(pseudo_grad[0], "rep")
    mean_delta = summed / groups
    mom_frag = lax.dynamic_slice_in_dim(momentum, frag_start, frag_w, 1)
    new_mom_frag = outer_momentum * mom_frag + mean_delta
    update = outer_rate * (outer_momentum * new_mom_frag + mean_delta)
    anchor_frag = lax.dynamic_slice_in_dim(anchor, frag_start, frag_w, 1)
    new_anchor = lax.dynamic_update_slice(anchor, anchor_frag - update, (zero_index, frag_start))
    new_momentum = lax.dynamic_update_slice(momentum, new_mom_frag, (zero_index, frag_start))
    narrow = master.astype(jnp.bfloat16)
    columns = tokens
    projected = jnp.dot(
        columns,
        lax.all_gather(narrow, "fsdp", axis=0, tiled=True),
        preferred_element_type=jnp.float32,
    )
    columns = tokens
    gradient = lax.psum_scatter(
        lax.dot_general(
            columns, grads_in, (((0,), (0,)), ((), ())), preferred_element_type=jnp.float32
        ),
        "fsdp",
        scatter_dimension=0,
        tiled=True,
    )
    moment_one = beta_one * first_moment[0] + (1.0 - beta_one) * gradient
    moment_two = beta_two * second_moment[0] + (1.0 - beta_two) * gradient * gradient
    stepped = master - inner_rate * (
        moment_one / (jnp.sqrt(moment_two) + adam_epsilon) + weight_decay * master
    )
    frag_cols = lax.dynamic_slice_in_dim(stepped, frag_start, frag_w, 1) + pseudo_grad[0] - update
    stepped = lax.dynamic_update_slice(stepped, frag_cols, (zero_index, frag_start))
    return (
        projected.astype(jnp.bfloat16)[None],
        stepped[None],
        moment_one[None],
        moment_two[None],
        new_anchor,
        new_momentum,
    )


def solution(mesh):
    return jax.shard_map(
        shards,
        mesh=mesh,
        in_specs=(
            P("rep", "fsdp", None),
            P("rep", "fsdp", None),
            P("rep", "fsdp", None),
            P("rep", "fsdp", None),
            P("rep", "fsdp", None),
            P("rep", "fsdp", None),
            P("fsdp", None),
            P("fsdp", None),
            P(),
        ),
        out_specs=(
            P("rep", "fsdp", None),
            P("rep", "fsdp", None),
            P("rep", "fsdp", None),
            P("rep", "fsdp", None),
            P("fsdp", None),
            P("fsdp", None),
        ),
        check_vma=False,
    )
```

profile of v0, /device:TPU:8, one launch (start us, length us, event | category | flops | bytes accessed | tf_op | source)
XLA Modules:
  0.0 899.0 jit_solution(3829941084241475924)
XLA Ops:
  8.0 0.0 copy-start
  8.0 0.0 all-gather.2.cloned.1.call-start
  8.1 1.1 copy.23
  9.1 1.8 bitcast_convert_fusion
  10.9 0.0 all-gather.2.cloned.1.call-update
  10.9 0.0 reduce-scatter.2.cloned.1.call-start
  11.0 0.0 copy-done
  11.0 11.1 %fusion = f32[8192,512]{1,0:T(8,128)} fusion(bf16[1,384,8192]{2,1,0:T(8,128)(2,1)} %param.9, bf16[1,384,512]{2,1,0:T(8,128)(2,1)S(1)} %copy-done), kind=kOutput, calls=%fused_computation | convolution fusion | flops 3221225472 | bytes 23461888 | tf_op jit(solution)/shard_map/dot_general | solution.py:42
  22.1 0.0 reduce-scatter.2.cloned.1.call-update
  22.1 0.0 all-reduce.2.cloned.1.call-start
  22.2 0.5 all-reduce.2.cloned.1.call-update
  23.4 0.0 copy-start.1
  23.4 0.0 copy-start.5
  23.4 0.0 copy-start.6
  23.4 0.0 copy-start.4
  23.4 144.8 %all-gather.2.cloned.1.call-done = bf16[8192,512]{1,0:T(8,128)(2,1)} async-done(((bf16[256,512]{1,0:T(8,128)(2,1)}), bf16[8192,512]{1,0:T(8,128)(2,1)}) %all-gather.2.cloned.1.call-update) | async-done | bytes 8388624 | tf_op jit(solution)/shard_map/all_gather | solution.py:37
  168.2 9.3 %fusion.7 = bf16[1,384,512]{2,1,0:T(8,128)(2,1)} fusion(bf16[8192,512]{1,0:T(8,128)(2,1)} %all-gather.2.cloned.1.call-done, bf16[1,384,8192]{2,1,0:T(8,128)(2,1)} %param.9), kind=kOutput, calls=%fused_computation.5 | convolution fusion | flops 3221422080 | bytes 15073280 | tf_op jit(solution)/shard_map/dot_general | solution.py:35
  177.5 708.4 %reduce-scatter.2.cloned.1.call-done = f32[256,512]{1,0:T(8,128)} async-done(((f32[8192,512]{1,0:T(8,128)}), f32[256,512]{1,0:T(8,128)}) %reduce-scatter.2.cloned.1.call-update) | async-done | bytes 524304 | tf_op jit(solution)/shard_map/reduce_scatter | solution.py:41
  885.9 0.0 copy-done.1
  885.9 0.0 copy-done.5
  885.9 0.0 copy-done.6
  885.9 2.4 fusion.15
  888.3 0.0 all-reduce.2.cloned.1.call-done
  888.4 1.0 bitcast_dynamic-update-slice_fusion
  889.4 0.0 copy-done.4
  889.4 0.0 copy-start.7
  889.4 1.1 fusion.16
  890.6 0.0 copy-start.2
  890.6 0.0 copy-start.3
  890.6 0.0 copy-done.7
  890.6 0.8 copy-done.2
  891.4 0.2 copy-done.3
  (1 shorter events, 0.0 us)
Async XLA Ops:
  8.0 3.0 copy-start
  8.0 160.2 %all-gather.2.cloned.1.call-start = ((), (), s32[]{:S(2)}) async-start(), calls=%async_computation.1 | async-start | bytes 8650752 | tf_op jit(solution)/shard_map/all_gather | solution.py:37
  10.9 875.0 %reduce-scatter.2.cloned.1.call-start = ((), (), s32[]{:S(2)}) async-start(), calls=%async_computation.2 | async-start | bytes 17301504 | tf_op jit(solution)/shard_map/reduce_scatter | solution.py:41
  22.1 866.2 %all-reduce.2.cloned.1.call-start = ((), (), s32[]{:S(2)}) async-start(), calls=%async_computation.3 | async-start | bytes 262144 | tf_op jit(solution)/shard_map/psum | solution.py:25
  23.4 862.6 %copy-start.1 = (f32[1,256,512]{2,1,0:T(8,128)S(1)}, f32[1,256,512]{2,1,0:T(8,128)}, u32[]{:S(2)}) copy-start(f32[1,256,512]{2,1,0:T(8,128)} %param.11) | copy-start | bytes 1572868
  23.4 862.5 %copy-start.5 = (f32[1,256,512]{2,1,0:T(8,128)S(1)}, f32[1,256,512]{2,1,0:T(8,128)}, u32[]{:S(2)}) copy-start(f32[1,256,512]{2,1,0:T(8,128)} %param.13) | copy-start | bytes 1572868
  23.4 862.5 %copy-start.6 = (f32[1,256,512]{2,1,0:T(8,128)S(1)}, f32[1,256,512]{2,1,0:T(8,128)}, u32[]{:S(2)}) copy-start(f32[1,256,512]{2,1,0:T(8,128)} %param.12) | copy-start | bytes 1572868
  23.4 866.0 %copy-start.4 = (f32[256,512]{1,0:T(8,128)S(1)}, f32[256,512]{1,0:T(8,128)}, u32[]{:S(2)}) copy-start(f32[256,512]{1,0:T(8,128)} %param.15) | copy-start | bytes 1572868
  889.4 1.2 copy-start.7
  890.6 0.8 copy-start.2
  890.6 1.0 copy-start.3
Sparse Core Ops, SparseCore 0:
  12.9 155.2 all-gather.1
  170.7 715.1 reduce-scatter.1
Sparse Core Ops, SparseCore 1:
  25.2 142.1 all-reduce.1
where the time goes:
time: 903 us; the launch traced here: 899 us
  waiting for transfers between devices  854 us (95%)
  matrix products  20.4 us (2%)
  between operations  16.3 us (2%)
    reduce_scatter x1, waiting for transfers between devices, shards(): lax.psum_scatter(lax.dot_general(columns, grads_in, (((0,), (0,)), ((), (...  708 us
    all_gather x1, waiting for transfers between devices, shards(): lax.all_gather(narrow, 'fsdp', axis=0, tiled=True)  145 us
  transfers between devices with their start and end apart: 3, of which 2 were waited for; matrix products, arithmetic and copies ran while one was open for 3% of the time, Pallas kernels for 0%

commit v1 on v0

v1 whole, which is shorter than its diff:
```python
import jax
import jax.numpy as jnp
from jax import lax
from jax.experimental import pallas as pl
from jax.experimental.pallas import tpu as pltpu
from jax.sharding import PartitionSpec as P

MESH = pl.DeviceIdType.MESH

beta_one = 0.9
beta_two = 0.95
inner_rate = 0.002
weight_decay = 0.1
adam_epsilon = 1e-08
outer_rate = 0.7
outer_momentum = 0.9

RING = 4
TWO = 2
PEERS = 8
COMBOS = RING * TWO
SIDE = 256

GATHER_ONE = 0
GATHER_TWO = GATHER_ONE + TWO * 2 * 4
REDUCE_ONE = GATHER_TWO + COMBOS * 2 * 4
REDUCE_TWO = REDUCE_ONE + COMBOS * 2 * 4
GATHER_Z = REDUCE_TWO + TWO * 2 * 4
REDUCE_Z = GATHER_Z + 2
PSUM_ONE = REDUCE_Z + 2
PSUM_TWO = PSUM_ONE + PEERS
N_SEMS = PSUM_TWO + PEERS

TOP = pl.ds(0, SIDE // 2)
LOW = pl.ds(SIDE // 2, SIDE // 2)
ALL = pl.ds(0, SIDE)
ROWS = (ALL, ALL, TOP, LOW)
STEP = (1, 3, 1, 3)


def gray(j):
    return j + j // 2 - 2 * (j // 2) * (j % 2)


def body(
    x_hbm, c_hbm, w_hbm, p_hbm, proj_ref, grad_ref, delta_ref,
    xb, cb, ct, wf, wg, acc, far, up, down, relay, sums, far2, up2, down2, relay2, sums2,
    zs, zr, grad_t, pg, pr, dl, load_sem, ss, rs,
):
    fsdp = lax.axis_index("fsdp")
    rep = lax.axis_index("rep")
    x, y, z = fsdp // 8, (fsdp // 2) % 4, fsdp % 2

    def place(h, first, second, zz):
        dx, dy = (first, second) if h == 0 else (second, first)
        return ((x + dx) % 4) * 8 + ((y + dy) % 4) * 2 + zz

    loads = [
        pltpu.make_async_copy(w_hbm, wf, load_sem.at[0]),
        pltpu.make_async_copy(c_hbm, cb, load_sem.at[1]),
        pltpu.make_async_copy(p_hbm, pg, load_sem.at[2]),
    ]
    for load in loads:
        load.start()

    @pl.loop(0, 32)
    def _(i):
        columns = pl.ds(pl.multiple_of(i * SIDE, SIDE), SIDE)
        pltpu.make_async_copy(x_hbm.at[:, columns], xb.at[i], load_sem.at[3]).start()

    barrier = pltpu.get_barrier_semaphore()
    near = [place(0, 1, 0, z), place(0, 3, 0, z), place(0, 0, 1, z), place(0, 0, 3, z), place(0, 0, 0, 1 - z)]
    for device in near:
        pl.semaphore_signal(barrier, inc=1, device_id={"fsdp": device}, device_id_type=MESH)
    for i in range(1, PEERS):
        pl.semaphore_signal(barrier, inc=1, device_id={"rep": (rep + i) % PEERS}, device_id_type=MESH)

    def send(src, dst, sem, device, axis="fsdp"):
        return pltpu.make_async_remote_copy(
            src_ref=src, dst_ref=dst, send_sem=ss.at[sem], recv_sem=rs.at[sem],
            device_id={axis: device}, device_id_type=MESH,
        )

    def ring(h, second, kind):
        return place(h, 0, STEP[kind], z) if second else place(h, STEP[kind], 0, z)

    def piece(f, h, kind):
        return wg.at[f, h, ROWS[kind]]

    def gather_copy(f, h, sem, kind, second):
        return send(piece(f, h, kind), piece(f, h, kind), sem + kind, ring(h, second, kind))

    def one_sem(r, h):
        return GATHER_ONE + (r * 2 + h) * 4

    def two_sem(a, h):
        return GATHER_TWO + (a * 2 + h) * 4

    def reduce_one_sem(c, h):
        return REDUCE_ONE + (c * 2 + h) * 4

    def reduce_two_sem(zi, h):
        return REDUCE_TWO + (zi * 2 + h) * 4

    def project(f, h):
        acc[h] += jnp.dot(xb[f], wg[f, h], preferred_element_type=jnp.float32)

    def gather_step(a):
        r, j = a // RING, a % RING
        zz = (z + r) % 2
        first = gray(j)
        for h in range(2):
            f = place(h, first, 0, zz)
            sem = one_sem(r, h)

            @pl.when(j == 0)
            def _():
                @pl.when(r == 1)
                def _():
                    send(wg.at[f, h], wg.at[f, h], GATHER_Z + h, place(0, 0, 0, 1 - z)).wait_recv()

                gather_copy(f, h, sem, 0, False).start()
                gather_copy(f, h, sem, 1, False).start()

            @pl.when(j == 1)
            def _():
                gather_copy(f, h, sem, 1, False).wait_recv()
                gather_copy(f, h, sem, 3, False).start()

            @pl.when(j == 2)
            def _():
                gather_copy(f, h, sem, 0, False).wait_recv()
                gather_copy(f, h, sem, 2, False).start()

            @pl.when(j == 3)
            def _():
                gather_copy(f, h, sem, 2, False).wait_recv()
                gather_copy(f, h, sem, 3, False).wait_recv()

            gather_copy(f, h, two_sem(a, h), 0, True).start()
            gather_copy(f, h, two_sem(a, h), 1, True).start()

    def gather_own(a):
        r, j = a // RING, a % RING
        for h in range(2):
            project(place(h, gray(j), 0, (z + r) % 2), h)

    def gather_forward(a):
        r, j = a // RING, a % RING
        zz = (z + r) % 2
        first = gray(j)
        for h in range(2):
            sem = two_sem(a, h)
            above, below = place(h, first, 1, zz), place(h, first, 3, zz)
            gather_copy(above, h, sem, 1, True).wait_recv()
            gather_copy(above, h, sem, 3, True).start()
            gather_copy(below, h, sem, 0, True).wait_recv()
            gather_copy(below, h, sem, 2, True).start()
        for h in range(2):
            project(place(h, first, 1, zz), h)
            project(place(h, first, 3, zz), h)

    def gather_last(a):
        r, j = a // RING, a % RING
        for h in range(2):
            f = place(h, gray(j), 2, (z + r) % 2)
            gather_copy(f, h, two_sem(a, h), 2, True).wait_recv()
            gather_copy(f, h, two_sem(a, h), 3, True).wait_recv()
            project(f, h)

    def partial(f, h):
        return jnp.dot(ct[h], xb[f], preferred_element_type=jnp.float32)

    def ring_copy(src, dst, h, sem, kind, second):
        return send(src.at[ROWS[kind]], dst.at[ROWS[kind]], sem + kind, ring(h, second, kind))

    def widen(value):
        return value.astype(jnp.float32)

    def narrow(value):
        return value.astype(jnp.bfloat16)

    def reduce_far(c):
        zi, j = c // RING, c % RING
        zz = (z + 1 + zi) % 2
        for h in range(2):
            far[c, h] = narrow(partial(place(h, gray(3 - j), 2, zz), h))
            sem = reduce_one_sem(c, h)
            ring_copy(far.at[c, h], relay.at[c, h], h, sem, 2, True).start()
            ring_copy(far.at[c, h], relay.at[c, h], h, sem, 3, True).start()

    def reduce_near(c):
        zi, j = c // RING, c % RING
        zz = (z + 1 + zi) % 2
        first = gray(3 - j)
        for h in range(2):
            sem = reduce_one_sem(c, h)
            value = partial(place(h, first, 1, zz), h)
            ring_copy(far.at[c, h], relay.at[c, h], h, sem, 2, True).wait_recv()
            up[c, h, TOP] = narrow(value[: SIDE // 2] + widen(relay[c, h, TOP]))
            up[c, h, LOW] = narrow(value[SIDE // 2 :])
            ring_copy(up.at[c, h], sums.at[c, h, 0], h, sem, 0, True).start()
            value = partial(place(h, first, 3, zz), h)
            ring_copy(far.at[c, h], relay.at[c, h], h, sem, 3, True).wait_recv()
            down[c, h, TOP] = narrow(value[: SIDE // 2])
            down[c, h, LOW] = narrow(value[SIDE // 2 :] + widen(relay[c, h, LOW]))
            ring_copy(down.at[c, h], sums.at[c, h, 1], h, sem, 1, True).start()

    def reduce_own(c):
        zi, j = c // RING, c % RING
        zz = (z + 1 + zi) % 2
        for h in range(2):
            sem = reduce_one_sem(c, h)
            sem2 = reduce_two_sem(zi, h)
            value = partial(place(h, gray(3 - j), 0, zz), h)
            ring_copy(up.at[c, h], sums.at[c, h, 0], h, sem, 0, True).wait_recv()
            ring_copy(down.at[c, h], sums.at[c, h, 1], h, sem, 1, True).wait_recv()
            value = value + widen(sums[c, h, 0]) + widen(sums[c, h, 1])

            @pl.when(j == 0)
            def _():
                far2[zi, h] = narrow(value)
                ring_copy(far2.at[zi, h], relay2.at[zi, h], h, sem2, 2, False).start()
                ring_copy(far2.at[zi, h], relay2.at[zi, h], h, sem2, 3, False).start()

            @pl.when(j == 1)
            def _():
                ring_copy(far2.at[zi, h], relay2.at[zi, h], h, sem2, 3, False).wait_recv()
                down2[zi, h, TOP] = narrow(value[: SIDE // 2])
                down2[zi, h, LOW] = narrow(value[SIDE // 2 :] + widen(relay2[zi, h, LOW]))
                ring_copy(down2.at[zi, h], sums2.at[zi, h, 1], h, sem2, 1, False).start()

            @pl.when(j == 2)
            def _():
                ring_copy(far2.at[zi, h], relay2.at[zi, h], h, sem2, 2, False).wait_recv()
                up2[zi, h, TOP] = narrow(value[: SIDE // 2] + widen(relay2[zi, h, TOP]))
                up2[zi, h, LOW] = narrow(value[SIDE // 2 :])
                ring_copy(up2.at[zi, h], sums2.at[zi, h, 0], h, sem2, 0, False).start()

            @pl.when(j == 3)
            def _():
                ring_copy(up2.at[zi, h], sums2.at[zi, h, 0], h, sem2, 0, False).wait_recv()
                ring_copy(down2.at[zi, h], sums2.at[zi, h, 1], h, sem2, 1, False).wait_recv()
                total = value + widen(sums2[zi, h, 0]) + widen(sums2[zi, h, 1])

                @pl.when(zi == 0)
                def _():
                    zs[h] = total
                    send(zs.at[h], zr.at[h], REDUCE_Z + h, place(0, 0, 0, 1 - z)).start()

                @pl.when(zi == 1)
                def _():
                    grad_t[h] = total

    share = SIDE // PEERS

    def share_of(device):
        return pl.ds(pl.multiple_of(device * share, share), share)

    def psum_one(i):
        peer = (rep + i) % PEERS
        return send(pg.at[share_of(peer)], pr.at[rep], PSUM_ONE + i, peer, "rep")

    def psum_two(i):
        peer = (rep + i) % PEERS
        return send(dl.at[share_of(rep)], dl.at[share_of(rep)], PSUM_TWO + i, peer, "rep")

    loads[0].wait()
    for h in range(2):
        wg[fsdp, h] = wf[:, h * SIDE : (h + 1) * SIDE].astype(jnp.bfloat16)
    pl.semaphore_wait(barrier, len(near) + PEERS - 1)
    for h in range(2):
        send(wg.at[fsdp, h], wg.at[fsdp, h], GATHER_Z + h, place(0, 0, 0, 1 - z)).start()
    gather_step(0)
    loads[2].wait()
    for i in range(1, PEERS):
        psum_one(i).start()
    loads[1].wait()
    for h in range(2):
        half = cb[:, h * SIDE : (h + 1) * SIDE].astype(jnp.float32)
        ct[h] = half.T.astype(jnp.bfloat16)
    acc[...] = jnp.zeros_like(acc)
    pltpu.make_async_copy(xb, xb, load_sem.at[3]).wait()

    @pl.loop(0, COMBOS + 2)
    def _(k):
        @pl.when(k < COMBOS)
        def _():
            reduce_far(k)

            @pl.when(k > 0)
            def _():
                gather_step(k)

            gather_own(k)

        @pl.when((k >= 1) & (k < COMBOS + 1))
        def _():
            reduce_near(k - 1)
            gather_forward(k - 1)

        @pl.when(k >= 2)
        def _():
            reduce_own(k - 2)
            gather_last(k - 2)

        @pl.when(k == 2)
        def _():
            pr[rep] = pg[share_of(rep)]
            for i in range(1, PEERS):
                psum_one(i).wait_recv()
            dl[share_of(rep)] = jnp.sum(pr[...], axis=0)
            for i in range(1, PEERS):
                psum_two(i).start()

    proj_ref[...] = jnp.concatenate([acc[0], acc[1]], axis=1).astype(jnp.bfloat16)
    for h in range(2):
        send(zs.at[h], zr.at[h], REDUCE_Z + h, place(0, 0, 0, 1 - z)).wait_recv()
        grad_ref[:, h * SIDE : (h + 1) * SIDE] = (grad_t[h] + zr[h]).T
    for i in range(1, PEERS):
        peer = (rep + PEERS - i) % PEERS
        send(dl.at[share_of(peer)], dl.at[share_of(peer)], PSUM_TWO + i, peer, "rep").wait_recv()
    delta_ref[...] = dl[...]

    for i in range(1, PEERS):
        psum_one(i).wait_send()
        psum_two(i).wait_send()
    for h in range(2):
        send(wg.at[fsdp, h], wg.at[fsdp, h], GATHER_Z + h, place(0, 0, 0, 1 - z)).wait_send()
        send(zs.at[h], zr.at[h], REDUCE_Z + h, place(0, 0, 0, 1 - z)).wait_send()

    @pl.loop(0, COMBOS)
    def _(c):
        for h in range(2):
            for kind in range(4):
                gather_copy(fsdp, h, two_sem(c, h), kind, True).wait_send()
                ring_copy(far.at[c, h], relay.at[c, h], h, reduce_one_sem(c, h), kind, True).wait_send()

    @pl.loop(0, TWO)
    def _(r):
        for h in range(2):
            for kind in range(4):
                gather_copy(fsdp, h, one_sem(r, h), kind, False).wait_send()
                ring_copy(far2.at[r, h], relay2.at[r, h], h, reduce_two_sem(r, h), kind, False).wait_send()


def exchange(tokens, grads_in, master, pseudo):
    n, depth = tokens.shape
    rows, width = master.shape
    bf16, f32 = jnp.bfloat16, jnp.float32
    square = (SIDE, SIDE)
    flops = 4 * n * depth * width
    return pl.pallas_call(
        body,
        out_shape=[
            jax.ShapeDtypeStruct((n, width), bf16),
            jax.ShapeDtypeStruct((rows, width), f32),
            jax.ShapeDtypeStruct(pseudo.shape, f32),
        ],
        in_specs=[pl.BlockSpec(memory_space=pl.ANY)] * 4,
        out_specs=[pl.BlockSpec(memory_space=pltpu.VMEM)] * 3,
        scratch_shapes=[
            pltpu.VMEM((32, n, SIDE), bf16),
            pltpu.VMEM((n, width), bf16),
            pltpu.VMEM((2, SIDE, n), bf16),
            pltpu.VMEM((rows, width), f32),
            pltpu.VMEM((32, 2) + square, bf16),
            pltpu.VMEM((2, n, SIDE), f32),
            pltpu.VMEM((COMBOS, 2) + square, bf16),
            pltpu.VMEM((COMBOS, 2) + square, bf16),
            pltpu.VMEM((COMBOS, 2) + square, bf16),
            pltpu.VMEM((COMBOS, 2) + square, bf16),
            pltpu.VMEM((COMBOS, 2, 2) + square, bf16),
            pltpu.VMEM((TWO, 2) + square, bf16),
            pltpu.VMEM((TWO, 2) + square, bf16),
            pltpu.VMEM((TWO, 2) + square, bf16),
            pltpu.VMEM((TWO, 2) + square, bf16),
            pltpu.VMEM((TWO, 2, 2) + square, bf16),
            pltpu.VMEM((2,) + square, f32),
            pltpu.VMEM((2,) + square, f32),
            pltpu.VMEM((2,) + square, f32),
            pltpu.VMEM(pseudo.shape, f32),
            pltpu.VMEM((PEERS, SIDE // PEERS, pseudo.shape[1]), f32),
            pltpu.VMEM(pseudo.shape, f32),
            pltpu.SemaphoreType.DMA((4,)),
            pltpu.SemaphoreType.DMA((N_SEMS,)),
            pltpu.SemaphoreType.DMA((N_SEMS,)),
        ],
        compiler_params=pltpu.CompilerParams(
            collective_id=0, has_side_effects=True, vmem_limit_bytes=58 * 2**20
        ),
        cost_estimate=pl.CostEstimate(flops=flops, bytes_accessed=12 * 2**20, transcendentals=0),
    )(tokens, grads_in, master, pseudo)


def shards(
    inputs, cotangent, weights, first_moment, second_moment, pseudo_grad, anchor, momentum, fragment
):
    master = weights[0]
    frag_w = pseudo_grad.shape[2]
    frag_start = fragment[0] * frag_w
    zero_index = jnp.zeros((), jnp.int32)
    groups = lax.axis_size("rep")
    projected, gradient, summed = exchange(inputs[0], cotangent[0], master, pseudo_grad[0])
    mean_delta = summed / groups
    mom_frag = lax.dynamic_slice_in_dim(momentum, frag_start, frag_w, 1)
    new_mom_frag = outer_momentum * mom_frag + mean_delta
    update = outer_rate * (outer_momentum * new_mom_frag + mean_delta)
    anchor_frag = lax.dynamic_slice_in_dim(anchor, frag_start, frag_w, 1)
    new_anchor = lax.dynamic_update_slice(anchor, anchor_frag - update, (zero_index, frag_start))
    new_momentum = lax.dynamic_update_slice(momentum, new_mom_frag, (zero_index, frag_start))
    moment_one = beta_one * first_moment[0] + (1.0 - beta_one) * gradient
    moment_two = beta_two * second_moment[0] + (1.0 - beta_two) * gradient * gradient
    stepped = master - inner_rate * (
        moment_one / (jnp.sqrt(moment_two) + adam_epsilon) + weight_decay * master
    )
    frag_cols = lax.dynamic_slice_in_dim(stepped, frag_start, frag_w, 1) + pseudo_grad[0] - update
    stepped = lax.dynamic_update_slice(stepped, frag_cols, (zero_index, frag_start))
    return (
        projected[None],
        stepped[None],
        moment_one[None],
        moment_two[None],
        new_anchor,
        new_momentum,
    )


def solution(mesh):
    return jax.shard_map(
        shards,
        mesh=mesh,
        in_specs=(
            P("rep", "fsdp", None),
            P("rep", "fsdp", None),
            P("rep", "fsdp", None),
            P("rep", "fsdp", None),
            P("rep", "fsdp", None),
            P("rep", "fsdp", None),
            P("fsdp", None),
            P("fsdp", None),
            P(),
        ),
        out_specs=(
            P("rep", "fsdp", None),
            P("rep", "fsdp", None),
            P("rep", "fsdp", None),
            P("rep", "fsdp", None),
            P("fsdp", None),
            P("fsdp", None),
        ),
        check_vma=False,
    )
```

time: 903 us -> 109 us (0.12)
  waiting for transfers between devices: 854 us -> 0 us
  Pallas kernels: 0 us -> 101 us
  matrix products: 20.4 us -> 0 us
  between operations: 16.3 us -> 1.43 us
    reduce_scatter x1 -> x0, waiting for transfers between devices: 708 us -> none  [shards(): lax.psum_scatter(lax.dot_general(columns, grads_in, (((0,), (0,)), ((), (...]
    all_gather x1 -> x0, waiting for transfers between devices: 145 us -> none  [shards(): lax.all_gather(narrow, 'fsdp', axis=0, tiled=True)]
    pallas_call x0 -> x1, Pallas kernels: none -> 101 us  [exchange(): pl.pallas_call(body, out_shape=[jax.ShapeDtypeStruct((n, width), bf16), j...]
    dot_general x2 -> x0, matrix products: 20.4 us -> none  [the longest x1 11.1 us: shards(): lax.dot_general(columns, grads_in, (((0,), (0,)), ((), ())), preferred_el...]
  transfers between devices with their start and end apart: 3 -> 0, of which waited for: 2 -> 0; matrix products, arithmetic and copies ran while one was open for 3% -> 0% of each run, Pallas kernels for 0% -> 0%
where the time goes in v1:
time: 109 us
  Pallas kernels  101 us (93%)
  other arithmetic  4.51 us (4%)
  local copies, waits for them, and re-layouts  2.19 us (2%)
  between operations  1.43 us (1%)
    pallas_call x1, Pallas kernels, exchange(): pl.pallas_call(body, out_shape=[jax.ShapeDtypeStruct((n, width), bf16), j...  101 us
    broadcast_in_dim x1, other arithmetic, shards(): moment_two[None]  2.41 us
    unnamed x21, local copies, waits for them, and re-layouts  2.19 us

profile of v1, /device:TPU:8, one launch (start us, length us, event | category | flops | bytes accessed | tf_op | source)
XLA Modules:
  0.0 109.1 jit_solution(13013993379213158139)
XLA Ops:
  0.6 1.0 copy.23
  2.3 0.0 copy-start.3
  2.3 0.0 copy-start.4
  2.4 0.0 copy-start.5
  2.4 0.0 copy-start.8
  2.4 0.0 copy-start.2
  2.4 100.9 %shard_map.136 = (bf16[384,512]{1,0:T(8,128)(2,1)}, f32[256,512]{1,0:T(8,128)}, f32[256,128]{1,0:T(8,128)}) custom-call(bf16[384,8192]{1,0:T(8,128)(2,1)} %bitcast.31, bf16[384,512]{1,0:T(8,128)(2,1)} %bitcast.32, f32[256,512]{1,0:T(8,128)} %bitcast.28, f32[256,128]{1,0:T(8,128)} %bitcast.30), custom_call_target="tpu_custom_call" | custom-call | flops 6442450944 | bytes 12582912 | tf_op jit(solution)/shard_map/pallas_call | solution.py:353
  103.3 0.0 copy-start.7
  103.3 0.0 copy-done.3
  103.4 0.0 copy-done.4
  103.4 0.0 copy-done.5
  103.4 2.4 %fusion.2 = (f32[1,256,512]{2,1,0:T(8,128)}, f32[256,512]{1,0:T(8,128)S(1)}, f32[1,256,512]{2,1,0:T(8,128)}) fusion(f32[256,512]{1,0:T(8,128)} %get-tuple-element.10, f32[1,256,512]{2,1,0:T(8,128)S(1)} %copy-done.4, f32[1,256,512]{2,1,0:T(8,128)S(1)} %copy-done.5, f32[1,256,512]{2,1,0:T(8,128)S(1)} %copy-done.3), kind=kLoop, calls=%fused_computation.5 | loop fusion | flops 1703936 | bytes 3670016 | tf_op jit(solution)/shard_map/broadcast_in_dim | solution.py:423
  105.8 0.0 copy-done.8
  105.8 1.0 bitcast_dynamic-update-slice_fusion
  106.8 0.0 copy-done.2
  106.8 0.0 copy-start.6
  106.8 1.1 %fusion.3 = (f32[256,512]{1,0:T(8,128)S(1)}, f32[256,512]{1,0:T(8,128)S(1)}) fusion(f32[256,512]{1,0:T(8,128)S(1)} %copy.23, s32[]{:T(128)S(6)} %select_n.2, f32[256,128]{1,0:T(8,128)} %get-tuple-element.11, f32[256,512]{1,0:T(8,128)S(1)} %copy-done.2), kind=kLoop, calls=%fused_computation.10 | loop fusion | flops 229376 | bytes 655364 | tf_op jit(solution)/shard_map/dynamic_update_slice | solution.py:411
  108.0 0.0 copy-start
  108.0 0.0 copy-start.1
  108.0 0.0 copy-done.7
  108.0 0.8 copy.24
  108.8 0.0 copy-done.6
  108.8 0.1 copy-done
  108.9 0.2 copy-done.1
  (1 shorter events, 0.0 us)
Async XLA Ops:
  2.3 101.0 %copy-start.3 = (f32[1,256,512]{2,1,0:T(8,128)S(1)}, f32[1,256,512]{2,1,0:T(8,128)}, u32[]{:S(2)}) copy-start(f32[1,256,512]{2,1,0:T(8,128)} %param.11) | copy-start | bytes 1572868
  2.3 101.0 %copy-start.4 = (f32[1,256,512]{2,1,0:T(8,128)S(1)}, f32[1,256,512]{2,1,0:T(8,128)}, u32[]{:S(2)}) copy-start(f32[1,256,512]{2,1,0:T(8,128)} %param.13) | copy-start | bytes 1572868
  2.4 101.0 %copy-start.5 = (f32[1,256,512]{2,1,0:T(8,128)S(1)}, f32[1,256,512]{2,1,0:T(8,128)}, u32[]{:S(2)}) copy-start(f32[1,256,512]{2,1,0:T(8,128)} %param.12) | copy-start | bytes 1572868
  2.4 103.5 %copy-start.8 = (f32[1,256,128]{2,1,0:T(8,128)S(1)}, f32[1,256,128]{2,1,0:T(8,128)}, u32[]{:S(2)}) copy-start(f32[1,256,128]{2,1,0:T(8,128)} %param.14) | copy-start | bytes 393220
  2.4 104.4 %copy-start.2 = (f32[256,512]{1,0:T(8,128)S(1)}, f32[256,512]{1,0:T(8,128)}, u32[]{:S(2)}) copy-start(f32[256,512]{1,0:T(8,128)} %param.15) | copy-start | bytes 1572868
  103.3 4.7 %copy-start.7 = (bf16[384,512]{1,0:T(8,128)(2,1)S(1)}, bf16[384,512]{1,0:T(8,128)(2,1)}, u32[]{:S(2)}) copy-start(bf16[384,512]{1,0:T(8,128)(2,1)} %get-tuple-element.9) | copy-start | bytes 1179652
  106.8 2.0 %copy-start.6 = (f32[1,256,512]{2,1,0:T(8,128)}, f32[1,256,512]{2,1,0:T(8,128)S(1)}, u32[]{:S(2)}) copy-start(f32[1,256,512]{2,1,0:T(8,128)S(1)} %bitcast_dynamic-update-slice_fusion) | copy-start | bytes 1572868
  108.0 0.9 copy-start
  108.0 1.1 copy-start.1

commit v2 on v0

v2 whole, which is shorter than its diff:
```python
import jax
import jax.numpy as jnp
from jax import lax
from jax.experimental import pallas as pl
from jax.experimental.pallas import tpu as pltpu
from jax.sharding import PartitionSpec as P

MESH = pl.DeviceIdType.MESH

beta_one = 0.9
beta_two = 0.95
inner_rate = 0.002
weight_decay = 0.1
adam_epsilon = 1e-08
outer_rate = 0.7
outer_momentum = 0.9

RING = 4
TWO = 2
PEERS = 8
COMBOS = RING * TWO
SIDE = 256
HALF = SIDE // 2
LAG = 3

GATHER_RING = 0
GATHER_CROSS = GATHER_RING + TWO * 2 * 4
TRADE = GATHER_CROSS + COMBOS * 2
TRADE_COT = TRADE + COMBOS * 2 * 2
REDUCE_CROSS = TRADE_COT + 2
REDUCE_RING = REDUCE_CROSS + COMBOS * 2
GATHER_Z = REDUCE_RING + TWO * 2 * 4
REDUCE_Z = GATHER_Z + 2
KEYS = REDUCE_Z + 2
PSUM_ONE = KEYS + 2
PSUM_TWO = PSUM_ONE + PEERS
N_SEMS = PSUM_TWO + PEERS

STEP = (1, 3, 1, 3)
OWN, CROSS, PAIR, PAIR_CROSS = range(4)


def gray(j):
    return j + j // 2 - 2 * (j // 2) * (j % 2)


def rows_of(kind, n):
    return (pl.ds(0, n), pl.ds(0, n), pl.ds(0, n // 2), pl.ds(n // 2, n // 2))[kind]


def body(
    x_hbm, c_hbm, w_hbm, p_hbm, proj_ref, grad_ref, delta_ref,
    xc, cb, ct, wf, wg, acc, acc_pair, keys, keys_in,
    cross, cross_in, far, up, down, relay, sums,
    zs, zr, grad_t, pg, pr, dl, load_sem, ss, rs,
):
    fsdp = lax.axis_index("fsdp")
    rep = lax.axis_index("rep")
    x, y, z = fsdp // 8, (fsdp // 2) % 4, fsdp % 2
    tokens, width = c_hbm.shape

    def along(at, who):
        pair = at + 1 - 2 * (at % 2)
        return (at, 3 - at, pair, 3 - pair)[who]

    def place(h, who, step, zz):
        if h == 0:
            return along(x, who) * 8 + ((y + step) % 4) * 2 + zz
        return ((x + step) % 4) * 8 + along(y, who) * 2 + zz

    other_z = fsdp + 1 - 2 * z

    def send(src, dst, sem, device, axis="fsdp"):
        return pltpu.make_async_remote_copy(
            src_ref=src, dst_ref=dst, send_sem=ss.at[sem], recv_sem=rs.at[sem],
            device_id={axis: device}, device_id_type=MESH,
        )

    def gather_round(a):
        return a // RING, a % RING, (z + a // RING) % 2, gray(a % RING)

    def reduce_round(c):
        return c // RING, c % RING, (z + 1 + c // RING) % 2, gray(3 - c % RING)

    load_w = pltpu.make_async_copy(w_hbm, wf, load_sem.at[0])
    load_c = pltpu.make_async_copy(c_hbm, cb.at[0], load_sem.at[1])
    load_p = pltpu.make_async_copy(p_hbm, pg, load_sem.at[2])
    load_w.start()
    load_c.start()
    load_p.start()

    def block(f, h):
        return x_hbm.at[:, pl.ds(pl.multiple_of(f * SIDE + h * HALF, HALF), HALF)]

    @pl.loop(0, COMBOS)
    def _(c):
        _, _, zz, step = reduce_round(c)
        for h in range(2):
            for who in (CROSS, OWN):
                f = place(h, who, step, zz)
                pltpu.make_async_copy(block(f, h), xc.at[f, h, pl.ds(0, tokens)], load_sem.at[3]).start()

    barrier = pltpu.get_barrier_semaphore()
    near = [place(0, PAIR, 0, z), place(0, CROSS, 0, z), place(1, PAIR, 0, z), place(1, CROSS, 0, z), other_z]
    for device in near:
        pl.semaphore_signal(barrier, inc=1, device_id={"fsdp": device}, device_id_type=MESH)
    for i in range(1, PEERS):
        pl.semaphore_signal(barrier, inc=1, device_id={"rep": (rep + i) % PEERS}, device_id_type=MESH)

    def trade_cot(h):
        return send(c_hbm, cb.at[1 + h], TRADE_COT + h, place(h, PAIR, 0, z))

    def trade_start(c):
        _, _, zz, step = reduce_round(c)
        for h in range(2):
            for i, who in enumerate((PAIR_CROSS, PAIR)):
                f = place(h, who, step, zz)
                sem = TRADE + (c * 2 + h) * 2 + i
                send(block(f, h), xc.at[f, h, pl.ds(tokens, tokens)], sem, place(h, PAIR, 0, z)).start()

    def trade_wait(c, h, i):
        _, _, zz, step = reduce_round(c)
        f = place(h, (CROSS, OWN)[i], step, zz)
        sem = TRADE + (c * 2 + h) * 2 + i
        send(block(f, h), xc.at[f, h, pl.ds(tokens, tokens)], sem, place(h, PAIR, 0, z)).wait_recv()

    def gather_ring(f, h, r, kind):
        part = wg.at[f, h, rows_of(kind, HALF)]
        return send(part, part, GATHER_RING + (r * 2 + h) * 4 + kind, place(h, OWN, STEP[kind], z))

    def gather_cross(f, h, a):
        return send(wg.at[f, h], wg.at[f, h], GATHER_CROSS + a * 2 + h, place(h, CROSS, 0, z))

    def gather_z(f, h):
        return send(wg.at[f, h], wg.at[f, h], GATHER_Z + h, other_z)

    def gather_step(a):
        r, j, zz, step = gather_round(a)
        for h in range(2):
            f = place(h, OWN, step, zz)

            @pl.when(j == 0)
            def _():
                @pl.when(r == 1)
                def _():
                    gather_z(f, h).wait_recv()

                gather_ring(f, h, r, 0).start()
                gather_ring(f, h, r, 1).start()

            @pl.when(j == 1)
            def _():
                gather_ring(f, h, r, 1).wait_recv()
                gather_ring(f, h, r, 3).start()

            @pl.when(j == 2)
            def _():
                gather_ring(f, h, r, 0).wait_recv()
                gather_ring(f, h, r, 2).start()

            @pl.when(j == 3)
            def _():
                gather_ring(f, h, r, 2).wait_recv()
                gather_ring(f, h, r, 3).wait_recv()

            gather_cross(f, h, a).start()

    def project(c):
        _, _, zz, step = reduce_round(c)
        for h in range(2):
            here, there = place(h, OWN, step, zz), place(h, CROSS, step, zz)
            gather_cross(there, h, COMBOS - 1 - c).wait_recv()
            value = jnp.dot(xc[here, h], wg[here, h], preferred_element_type=jnp.float32)
            value += jnp.dot(xc[there, h], wg[there, h], preferred_element_type=jnp.float32)
            acc[...] += value[:tokens]
            acc_pair[h] += value[tokens:]

    def keys_copy(h):
        return send(keys.at[h], keys_in.at[h], KEYS + h, place(h, PAIR, 0, z))

    def partial(f, h):
        return jnp.dot(ct[h], xc[f, h], preferred_element_type=jnp.float32)

    def widen(value):
        return value.astype(jnp.float32)

    def narrow(value):
        return value.astype(jnp.bfloat16)

    def reduce_cross(c, h):
        return send(cross.at[c, h], cross_in.at[c, h], REDUCE_CROSS + c * 2 + h, place(h, CROSS, 0, z))

    def reduce_ring(src, dst, zi, h, kind):
        rows = rows_of(kind, width)
        sem = REDUCE_RING + (zi * 2 + h) * 4 + kind
        return send(src.at[zi, h, rows], dst.at[rows], sem, place(h, OWN, STEP[kind], z))

    def relay_copy(zi, h, kind):
        return reduce_ring(far, relay.at[zi, h], zi, h, kind)

    def up_copy(zi, h):
        return reduce_ring(up, sums.at[zi, h, 0], zi, h, 0)

    def down_copy(zi, h):
        return reduce_ring(down, sums.at[zi, h, 1], zi, h, 1)

    def reduce_z(h):
        return send(zs.at[h], zr.at[h], REDUCE_Z + h, other_z)

    def reduce_first(c):
        _, _, zz, step = reduce_round(c)
        for h in range(2):
            trade_wait(c, h, 0)
            trade_wait(c, h, 1)
            cross[c, h] = narrow(partial(place(h, CROSS, step, zz), h))
            reduce_cross(c, h).start()

    def reduce_second(c):
        zi, j, zz, step = reduce_round(c)
        top, low = slice(0, width // 2), slice(width // 2, width)
        for h in range(2):
            value = partial(place(h, OWN, step, zz), h)
            reduce_cross(c, h).wait_recv()
            value = value + widen(cross_in[c, h])

            @pl.when(j == 0)
            def _():
                far[zi, h] = narrow(value)
                relay_copy(zi, h, 2).start()
                relay_copy(zi, h, 3).start()

            @pl.when(j == 1)
            def _():
                relay_copy(zi, h, 3).wait_recv()
                down[zi, h, top] = narrow(value[top])
                down[zi, h, low] = narrow(value[low] + widen(relay[zi, h, low]))
                down_copy(zi, h).start()

            @pl.when(j == 2)
            def _():
                relay_copy(zi, h, 2).wait_recv()
                up[zi, h, top] = narrow(value[top] + widen(relay[zi, h, top]))
                up[zi, h, low] = narrow(value[low])
                up_copy(zi, h).start()

            @pl.when(j == 3)
            def _():
                up_copy(zi, h).wait_recv()
                down_copy(zi, h).wait_recv()
                total = value + widen(sums[zi, h, 0]) + widen(sums[zi, h, 1])

                @pl.when(zi == 0)
                def _():
                    zs[h] = total
                    reduce_z(h).start()

                @pl.when(zi == 1)
                def _():
                    grad_t[h] = total

    share = SIDE // PEERS

    def share_of(device):
        return pl.ds(pl.multiple_of(device * share, share), share)

    def psum_one(i):
        peer = (rep + i) % PEERS
        return send(pg.at[share_of(peer)], pr.at[rep], PSUM_ONE + i, peer, "rep")

    def psum_two(i):
        peer = (rep + i) % PEERS
        return send(dl.at[share_of(rep)], dl.at[share_of(rep)], PSUM_TWO + i, peer, "rep")

    pl.semaphore_wait(barrier, len(near) + PEERS - 1)
    trade_cot(0).start()
    trade_cot(1).start()
    trade_start(0)
    load_w.wait()
    for h in range(2):
        wg[fsdp, h] = narrow(wf[h * HALF : (h + 1) * HALF])
    for h in range(2):
        gather_z(fsdp, h).start()
    gather_step(0)
    trade_start(1)
    load_p.wait()
    for i in range(1, PEERS):
        psum_one(i).start()
    acc[...] = jnp.zeros_like(acc)
    acc_pair[...] = jnp.zeros_like(acc_pair)
    load_c.wait()
    turned = narrow(widen(cb[0]).T)
    ct[0, :, 0:tokens] = turned
    ct[1, :, 0:tokens] = turned
    pltpu.make_async_copy(
        xc.at[pl.ds(0, 16), :, pl.ds(0, tokens)], xc.at[pl.ds(0, 16), :, pl.ds(0, tokens)], load_sem.at[3]
    ).wait()

    @pl.loop(1, COMBOS + LAG + 1)
    def _(k):
        @pl.when(k < COMBOS)
        def _():
            gather_step(k)

        @pl.when((k >= LAG) & (k < COMBOS + 1))
        def _():
            trade_start(k - LAG + 2)

        @pl.when(k == 2)
        def _():
            pr[rep] = pg[share_of(rep)]
            for i in range(1, PEERS):
                psum_one(i).wait_recv()
            dl[share_of(rep)] = jnp.sum(pr[...], axis=0)
            for i in range(1, PEERS):
                psum_two(i).start()
            for h in range(2):
                trade_cot(h).wait_recv()
                ct[h, :, tokens : 2 * tokens] = narrow(widen(cb[1 + h]).T)

        @pl.when((k >= LAG) & (k < COMBOS + LAG))
        def _():
            reduce_first(k - LAG)

        @pl.when(k >= LAG + 1)
        def _():
            reduce_second(k - LAG - 1)

        @pl.when((k >= LAG + 3) & (k < COMBOS + LAG))
        def _():
            project(k - LAG)

        @pl.when((k >= LAG + 4) & (k < LAG + 7))
        def _():
            project(LAG + 6 - k)

        @pl.when(k == COMBOS + LAG - 1)
        def _():
            for h in range(2):
                keys[h] = narrow(acc_pair[h])
                keys_copy(h).start()

    for h in range(2):
        reduce_z(h).wait_recv()
        grad_ref[h * HALF : (h + 1) * HALF] = (grad_t[h] + zr[h]).T
    for i in range(1, PEERS):
        peer = (rep + PEERS - i) % PEERS
        send(dl.at[share_of(peer)], dl.at[share_of(peer)], PSUM_TWO + i, peer, "rep").wait_recv()
    delta_ref[...] = dl[...]
    keys_copy(0).wait_recv()
    keys_copy(1).wait_recv()
    proj_ref[...] = narrow(acc[...] + widen(keys_in[0]) + widen(keys_in[1]))

    for i in range(1, PEERS):
        psum_one(i).wait_send()
        psum_two(i).wait_send()
    for h in range(2):
        gather_z(fsdp, h).wait_send()
        reduce_z(h).wait_send()
        keys_copy(h).wait_send()
        trade_cot(h).wait_send()

    @pl.loop(0, COMBOS)
    def _(c):
        for h in range(2):
            gather_cross(fsdp, h, c).wait_send()
            reduce_cross(c, h).wait_send()
            for i in range(2):
                sem = TRADE + (c * 2 + h) * 2 + i
                send(block(0, h), xc.at[fsdp, h, pl.ds(tokens, tokens)], sem, other_z).wait_send()

    @pl.loop(0, TWO)
    def _(r):
        for h in range(2):
            for kind in range(4):
                gather_ring(fsdp, h, r, kind).wait_send()
                reduce_ring(far, relay.at[r, h], r, h, kind).wait_send()


def exchange(tokens, grads_in, master, pseudo):
    n, depth = tokens.shape
    rows, width = master.shape
    bf16, f32 = jnp.bfloat16, jnp.float32
    tall = (width, HALF)
    flops = 4 * n * depth * width
    return pl.pallas_call(
        body,
        out_shape=[
            jax.ShapeDtypeStruct((n, width), bf16),
            jax.ShapeDtypeStruct((rows, width), f32),
            jax.ShapeDtypeStruct(pseudo.shape, f32),
        ],
        in_specs=[pl.BlockSpec(memory_space=pl.ANY)] * 4,
        out_specs=[pl.BlockSpec(memory_space=pltpu.VMEM)] * 3,
        scratch_shapes=[
            pltpu.VMEM((32, 2, 2 * n, HALF), bf16),
            pltpu.VMEM((3, n, width), bf16),
            pltpu.VMEM((2, width, 2 * n), bf16),
            pltpu.VMEM((rows, width), f32),
            pltpu.VMEM((32, 2, HALF, width), bf16),
            pltpu.VMEM((n, width), f32),
            pltpu.VMEM((2, n, width), f32),
            pltpu.VMEM((2, n, width), bf16),
            pltpu.VMEM((2, n, width), bf16),
            pltpu.VMEM((COMBOS, 2) + tall, bf16),
            pltpu.VMEM((COMBOS, 2) + tall, bf16),
            pltpu.VMEM((TWO, 2) + tall, bf16),
            pltpu.VMEM((TWO, 2) + tall, bf16),
            pltpu.VMEM((TWO, 2) + tall, bf16),
            pltpu.VMEM((TWO, 2) + tall, bf16),
            pltpu.VMEM((TWO, 2, 2) + tall, bf16),
            pltpu.VMEM((2,) + tall, f32),
            pltpu.VMEM((2,) + tall, f32),
            pltpu.VMEM((2,) + tall, f32),
            pltpu.VMEM(pseudo.shape, f32),
            pltpu.VMEM((PEERS, SIDE // PEERS, pseudo.shape[1]), f32),
            pltpu.VMEM(pseudo.shape, f32),
            pltpu.SemaphoreType.DMA((4,)),
            pltpu.SemaphoreType.DMA((N_SEMS,)),
            pltpu.SemaphoreType.DMA((N_SEMS,)),
        ],
        compiler_params=pltpu.CompilerParams(
            collective_id=0, has_side_effects=True, vmem_limit_bytes=58 * 2**20
        ),
        cost_estimate=pl.CostEstimate(flops=flops, bytes_accessed=12 * 2**20, transcendentals=0),
    )(tokens, grads_in, master, pseudo)


def shards(
    inputs, cotangent, weights, first_moment, second_moment, pseudo_grad, anchor, momentum, fragment
):
    master = weights[0]
    frag_w = pseudo_grad.shape[2]
    frag_start = fragment[0] * frag_w
    zero_index = jnp.zeros((), jnp.int32)
    groups = lax.axis_size("rep")
    projected, gradient, summed = exchange(inputs[0], cotangent[0], master, pseudo_grad[0])
    mean_delta = summed / groups
    mom_frag = lax.dynamic_slice_in_dim(momentum, frag_start, frag_w, 1)
    new_mom_frag = outer_momentum * mom_frag + mean_delta
    update = outer_rate * (outer_momentum * new_mom_frag + mean_delta)
    anchor_frag = lax.dynamic_slice_in_dim(anchor, frag_start, frag_w, 1)
    new_anchor = lax.dynamic_update_slice(anchor, anchor_frag - update, (zero_index, frag_start))
    new_momentum = lax.dynamic_update_slice(momentum, new_mom_frag, (zero_index, frag_start))
    moment_one = beta_one * first_moment[0] + (1.0 - beta_one) * gradient
    moment_two = beta_two * second_moment[0] + (1.0 - beta_two) * gradient * gradient
    stepped = master - inner_rate * (
        moment_one / (jnp.sqrt(moment_two) + adam_epsilon) + weight_decay * master
    )
    frag_cols = lax.dynamic_slice_in_dim(stepped, frag_start, frag_w, 1) + pseudo_grad[0] - update
    stepped = lax.dynamic_update_slice(stepped, frag_cols, (zero_index, frag_start))
    return (
        projected[None],
        stepped[None],
        moment_one[None],
        moment_two[None],
        new_anchor,
        new_momentum,
    )


def solution(mesh):
    return jax.shard_map(
        shards,
        mesh=mesh,
        in_specs=(
            P("rep", "fsdp", None),
            P("rep", "fsdp", None),
            P("rep", "fsdp", None),
            P("rep", "fsdp", None),
            P("rep", "fsdp", None),
            P("rep", "fsdp", None),
            P("fsdp", None),
            P("fsdp", None),
            P(),
        ),
        out_specs=(
            P("rep", "fsdp", None),
            P("rep", "fsdp", None),
            P("rep", "fsdp", None),
            P("rep", "fsdp", None),
            P("fsdp", None),
            P("fsdp", None),
        ),
        check_vma=False,
    )
```

time: 903 us -> 105 us (0.12)
  waiting for transfers between devices: 854 us -> 0 us
  Pallas kernels: 0 us -> 96.8 us
  matrix products: 20.4 us -> 0 us
  between operations: 16.3 us -> 1.43 us
    reduce_scatter x1 -> x0, waiting for transfers between devices: 708 us -> none  [shards(): lax.psum_scatter(lax.dot_general(columns, grads_in, (((0,), (0,)), ((), (...]
    all_gather x1 -> x0, waiting for transfers between devices: 145 us -> none  [shards(): lax.all_gather(narrow, 'fsdp', axis=0, tiled=True)]
    pallas_call x0 -> x1, Pallas kernels: none -> 96.8 us  [exchange(): pl.pallas_call(body, out_shape=[jax.ShapeDtypeStruct((n, width), bf16), j...]
    dot_general x2 -> x0, matrix products: 20.4 us -> none  [the longest x1 11.1 us: shards(): lax.dot_general(columns, grads_in, (((0,), (0,)), ((), ())), preferred_el...]
  transfers between devices with their start and end apart: 3 -> 0, of which waited for: 2 -> 0; matrix products, arithmetic and copies ran while one was open for 3% -> 0% of each run, Pallas kernels for 0% -> 0%
where the time goes in v2:
time: 105 us
  Pallas kernels  96.8 us (92%)
  other arithmetic  4.51 us (4%)
  local copies, waits for them, and re-layouts  2.19 us (2%)
  between operations  1.43 us (1%)
    pallas_call x1, Pallas kernels, exchange(): pl.pallas_call(body, out_shape=[jax.ShapeDtypeStruct((n, width), bf16), j...  96.8 us
    broadcast_in_dim x1, other arithmetic, shards(): moment_two[None]  2.41 us
    unnamed x21, local copies, waits for them, and re-layouts  2.19 us

profile of v2, /device:TPU:8, one launch (start us, length us, event | category | flops | bytes accessed | tf_op | source)
XLA Modules:
  0.0 105.0 jit_solution(7732582227545532177)
XLA Ops:
  0.6 1.0 copy.23
  2.3 0.0 copy-start.3
  2.3 0.0 copy-start.4
  2.4 0.0 copy-start.5
  2.4 0.0 copy-start.8
  2.4 0.0 copy-start.2
  2.4 96.8 %shard_map.136 = (bf16[384,512]{1,0:T(8,128)(2,1)}, f32[256,512]{1,0:T(8,128)}, f32[256,128]{1,0:T(8,128)}) custom-call(bf16[384,8192]{1,0:T(8,128)(2,1)} %bitcast.31, bf16[384,512]{1,0:T(8,128)(2,1)} %bitcast.32, f32[256,512]{1,0:T(8,128)} %bitcast.28, f32[256,128]{1,0:T(8,128)} %bitcast.30), custom_call_target="tpu_custom_call" | custom-call | flops 6442450944 | bytes 12582912 | tf_op jit(solution)/shard_map/pallas_call | solution.py:385
  99.2 0.0 copy-start.7
  99.2 0.0 copy-done.3
  99.2 0.0 copy-done.4
  99.3 0.0 copy-done.5
  99.3 2.4 %fusion.2 = (f32[1,256,512]{2,1,0:T(8,128)}, f32[256,512]{1,0:T(8,128)S(1)}, f32[1,256,512]{2,1,0:T(8,128)}) fusion(f32[256,512]{1,0:T(8,128)} %get-tuple-element.10, f32[1,256,512]{2,1,0:T(8,128)S(1)} %copy-done.4, f32[1,256,512]{2,1,0:T(8,128)S(1)} %copy-done.5, f32[1,256,512]{2,1,0:T(8,128)S(1)} %copy-done.3), kind=kLoop, calls=%fused_computation.5 | loop fusion | flops 1703936 | bytes 3670016 | tf_op jit(solution)/shard_map/broadcast_in_dim | solution.py:455
  101.7 0.0 copy-done.8
  101.7 1.0 bitcast_dynamic-update-slice_fusion
  102.7 0.0 copy-done.2
  102.7 0.0 copy-start.6
  102.7 1.1 %fusion.3 = (f32[256,512]{1,0:T(8,128)S(1)}, f32[256,512]{1,0:T(8,128)S(1)}) fusion(f32[256,512]{1,0:T(8,128)S(1)} %copy.23, s32[]{:T(128)S(6)} %select_n.2, f32[256,128]{1,0:T(8,128)} %get-tuple-element.11, f32[256,512]{1,0:T(8,128)S(1)} %copy-done.2), kind=kLoop, calls=%fused_computation.10 | loop fusion | flops 229376 | bytes 655364 | tf_op jit(solution)/shard_map/dynamic_update_slice | solution.py:443
  103.9 0.0 copy-start
  103.9 0.0 copy-start.1
  103.9 0.0 copy-done.7
  103.9 0.8 copy.24
  104.7 0.0 copy-done.6
  104.7 0.1 copy-done
  104.8 0.2 copy-done.1
  (1 shorter events, 0.0 us)
Async XLA Ops:
  2.3 96.9 %copy-start.3 = (f32[1,256,512]{2,1,0:T(8,128)S(1)}, f32[1,256,512]{2,1,0:T(8,128)}, u32[]{:S(2)}) copy-start(f32[1,256,512]{2,1,0:T(8,128)} %param.11) | copy-start | bytes 1572868
  2.3 96.9 %copy-start.4 = (f32[1,256,512]{2,1,0:T(8,128)S(1)}, f32[1,256,512]{2,1,0:T(8,128)}, u32[]{:S(2)}) copy-start(f32[1,256,512]{2,1,0:T(8,128)} %param.13) | copy-start | bytes 1572868
  2.4 96.9 %copy-start.5 = (f32[1,256,512]{2,1,0:T(8,128)S(1)}, f32[1,256,512]{2,1,0:T(8,128)}, u32[]{:S(2)}) copy-start(f32[1,256,512]{2,1,0:T(8,128)} %param.12) | copy-start | bytes 1572868
  2.4 99.3 %copy-start.8 = (f32[1,256,128]{2,1,0:T(8,128)S(1)}, f32[1,256,128]{2,1,0:T(8,128)}, u32[]{:S(2)}) copy-start(f32[1,256,128]{2,1,0:T(8,128)} %param.14) | copy-start | bytes 393220
  2.4 100.3 %copy-start.2 = (f32[256,512]{1,0:T(8,128)S(1)}, f32[256,512]{1,0:T(8,128)}, u32[]{:S(2)}) copy-start(f32[256,512]{1,0:T(8,128)} %param.15) | copy-start | bytes 1572868
  99.2 4.7 %copy-start.7 = (bf16[384,512]{1,0:T(8,128)(2,1)S(1)}, bf16[384,512]{1,0:T(8,128)(2,1)}, u32[]{:S(2)}) copy-start(bf16[384,512]{1,0:T(8,128)(2,1)} %get-tuple-element.9) | copy-start | bytes 1179652
  102.7 2.0 %copy-start.6 = (f32[1,256,512]{2,1,0:T(8,128)}, f32[1,256,512]{2,1,0:T(8,128)S(1)}, u32[]{:S(2)}) copy-start(f32[1,256,512]{2,1,0:T(8,128)S(1)} %bitcast_dynamic-update-slice_fusion) | copy-start | bytes 1572868
  103.9 0.9 copy-start
  103.9 1.1 %copy-start.1 = (f32[256,512]{1,0:T(8,128)}, f32[256,512]{1,0:T(8,128)S(1)}, u32[]{:S(2)}) copy-start(f32[256,512]{1,0:T(8,128)S(1)} %get-tuple-element.27) | copy-start | bytes 1572868

commit v3 on v0

v3 whole, which is shorter than its diff:
```python
import jax
import jax.numpy as jnp
from jax import lax
from jax.experimental import pallas as pl
from jax.experimental.pallas import tpu as pltpu
from jax.sharding import PartitionSpec as P

MESH = pl.DeviceIdType.MESH

beta_one = 0.9
beta_two = 0.95
inner_rate = 0.002
weight_decay = 0.1
adam_epsilon = 1e-08
outer_rate = 0.7
outer_momentum = 0.9

RING = 4
TWO = 2
PEERS = 8
COMBOS = RING * TWO
SIDE = 256
HALF = SIDE // 2
COT_PARTS = 3
FINISH_STEPS = 2

OWN, PAIR, FAR, CROSS = range(4)
GATHER_ORDER = (OWN, CROSS, PAIR, FAR)
VIA = (CROSS, CROSS)
BY_Z = (PAIR, FAR)
Z_DTYPE = jnp.float32

GATHER_RING = 0
GATHER_CROSS = GATHER_RING + TWO * RING * 2
GATHER_Z = GATHER_CROSS + TWO * RING * 2
TRADE = GATHER_Z + RING * 2
TRADE_COT = TRADE + COMBOS * 2 * 2
REDUCE_CROSS = TRADE_COT + 2 * COT_PARTS
REDUCE_RING = REDUCE_CROSS + COMBOS * 2
REDUCE_Z = REDUCE_RING + TWO * 2 * 3
KEYS = REDUCE_Z + 2
PSUM_ONE = KEYS + 2
PSUM_TWO = PSUM_ONE + PEERS
N_SEMS = PSUM_TWO + PEERS

PLAN = (
    "C1", "G1", "T0", "G2", "C2", "G3", "T1", "G4", "T2", "T3", "L0", "W0", "T4", "G5", "F0", "T5",
    "F1", "S0", "F2", "F3", "P1", "S1", "R0", "P3", "S2", "G6", "T6", "G7", "P4", "F4", "P5", "S3",
    "T7", "F5", "P2", "F6", "P6", "P0", "P7", "K0", "S4", "S5", "S6", "F7", "S7",
)


def flip(at, where):
    return (at, at + 1 - 2 * (at % 2), (at + 2) % 4, 3 - at)[where]


def body(
    x_hbm, c_hbm, w_hbm, p_hbm, proj_ref, grad_ref, delta_ref,
    xc, cb, ct, wf, wg, acc, acc_pair, keys, keys_in,
    cross, cross_in, around, around_in,
    zs, zr, grad_t, pg, pr, dl, load_sem, ss, rs,
):
    fsdp = lax.axis_index("fsdp")
    rep = lax.axis_index("rep")
    x, y, z = fsdp // 8, (fsdp // 2) % 4, fsdp % 2
    tokens, width = c_hbm.shape

    def place(h, first, second, zz):
        dx, dy = (first, second) if h == 0 else (second, first)
        return flip(x, dx) * 8 + flip(y, dy) * 2 + zz

    other_z = fsdp + 1 - 2 * z

    def send(src, dst, sem, device, axis="fsdp"):
        return pltpu.make_async_remote_copy(
            src_ref=src, dst_ref=dst, send_sem=ss.at[sem], recv_sem=rs.at[sem],
            device_id={axis: device}, device_id_type=MESH,
        )

    def reduce_round(c):
        zi, j = divmod(c, RING)
        other = PAIR + CROSS - VIA[zi]
        return zi, j, (z + 1 + zi) % 2, (FAR, VIA[zi], other, OWN)[j]

    load_w = pltpu.make_async_copy(w_hbm, wf, load_sem.at[0])
    load_c = pltpu.make_async_copy(c_hbm, cb.at[0], load_sem.at[1])
    load_p = pltpu.make_async_copy(p_hbm, pg, load_sem.at[2])
    load_w.start()
    load_c.start()
    load_p.start()

    barrier = pltpu.get_barrier_semaphore()
    near = [place(0, PAIR, OWN, z), place(0, CROSS, OWN, z), place(1, PAIR, OWN, z), place(1, CROSS, OWN, z), other_z]
    for device in near:
        pl.semaphore_signal(barrier, inc=1, device_id={"fsdp": device}, device_id_type=MESH)
    for i in range(1, PEERS):
        pl.semaphore_signal(barrier, inc=1, device_id={"rep": (rep + i) % PEERS}, device_id_type=MESH)

    def block(f, h):
        return x_hbm.at[:, pl.ds(pl.multiple_of(f * SIDE + h * HALF, HALF), HALF)]

    for c in range(COMBOS):
        _, _, zz, there = reduce_round(c)
        for h in range(2):
            for who in (CROSS, OWN):
                f = place(h, who, there, zz)
                pltpu.make_async_copy(block(f, h), xc.at[f, h, pl.ds(0, tokens)], load_sem.at[3]).start()

    def trade_cot(h, part):
        rows = pl.ds(part * HALF, HALF)
        return send(c_hbm.at[rows], cb.at[1 + h, rows], TRADE_COT + h * COT_PARTS + part, place(h, PAIR, OWN, z))

    def cot_start(part):
        for h in range(2):
            trade_cot(h, part).start()

    def cot_wait(_):
        for h in range(2):
            for part in range(COT_PARTS):
                trade_cot(h, part).wait_recv()
            ct[h, :, tokens : 2 * tokens] = narrow(widen(cb[1 + h]).T)

    def trade(c, h, i, who):
        _, _, zz, there = reduce_round(c)
        f = place(h, who, there, zz)
        sem = TRADE + (c * 2 + h) * 2 + i
        return send(block(f, h), xc.at[f, h, pl.ds(tokens, tokens)], sem, place(h, PAIR, OWN, z))

    def trade_start(c):
        for h in range(2):
            trade(c, h, 0, FAR).start()
            trade(c, h, 1, PAIR).start()

    arrived = set()

    def need(c, h, i):
        if (c, h, i) not in arrived:
            trade(c, h, i, (CROSS, OWN)[i]).wait_recv()
            arrived.add((c, h, i))

    def gather_ring(r, h, f, where, to):
        return send(wg.at[f, h], wg.at[f, h], GATHER_RING + (r * RING + where) * 2 + h, place(h, OWN, to, z))

    def gather_cross(r, h, f, where):
        return send(wg.at[f, h], wg.at[f, h], GATHER_CROSS + (r * RING + where) * 2 + h, place(h, CROSS, OWN, z))

    def gather_z(h, f, where):
        return send(wg.at[f, h], wg.at[f, h], GATHER_Z + where * 2 + h, other_z)

    def gather_step(a):
        r, j = divmod(a, RING)
        where = GATHER_ORDER[j]
        for h in range(2):
            f = place(h, OWN, where, (z + r) % 2)
            if r == 1 and (where == OWN or where in BY_Z):
                gather_z(h, f, where).wait_recv()
            elif where != OWN:
                gather_ring(r, h, f, where, PAIR).wait_recv()
            if where == OWN:
                for to in (PAIR, CROSS):
                    if r == 0 or to not in BY_Z:
                        gather_ring(r, h, f, to, to).start()
            elif where == CROSS and (r == 0 or FAR not in BY_Z):
                gather_ring(r, h, f, FAR, PAIR + CROSS - where).start()
            if r == 0 and (where == OWN or where in BY_Z):
                gather_z(h, f, where).start()
            gather_cross(r, h, f, where).start()

    seen = []

    def project(c):
        zi, _, zz, there = reduce_round(c)
        for h in range(2):
            mine, crossed = place(h, OWN, there, zz), place(h, CROSS, there, zz)
            need(c, h, 0)
            need(c, h, 1)
            gather_cross(1 - zi, h, crossed, there).wait_recv()
            value = jnp.dot(xc[mine, h], wg[mine, h], preferred_element_type=jnp.float32)
            value += jnp.dot(xc[crossed, h], wg[crossed, h], preferred_element_type=jnp.float32)
            acc[...] = value[:tokens] + acc[...] if seen else value[:tokens]
            acc_pair[h] = value[tokens:] + acc_pair[h] if len(seen) > 1 else value[tokens:]
            seen.append(c)

    def keys_copy(h):
        return send(keys.at[h], keys_in.at[h], KEYS + h, place(h, PAIR, OWN, z))

    def keys_start(_):
        for h in range(2):
            keys[h] = narrow(acc_pair[h])
            keys_copy(h).start()

    def partial(f, h):
        return jnp.dot(ct[h], xc[f, h], preferred_element_type=jnp.float32)

    def widen(value):
        return value.astype(jnp.float32)

    def narrow(value):
        return value.astype(jnp.bfloat16)

    def reduce_cross(c, h):
        return send(cross.at[c, h], cross_in.at[c, h], REDUCE_CROSS + c * 2 + h, place(h, CROSS, OWN, z))

    def reduce_ring(zi, h, j, to):
        slot = (zi, h, j)
        return send(around.at[slot], around_in.at[slot], REDUCE_RING + (zi * 2 + h) * 3 + j, place(h, OWN, to, z))

    def reduce_z(h):
        return send(zs.at[h], zr.at[h], REDUCE_Z + h, other_z)

    def reduce_first(c):
        _, _, zz, there = reduce_round(c)
        for h in range(2):
            need(c, h, 0)
            cross[c, h] = narrow(partial(place(h, CROSS, there, zz), h))
            reduce_cross(c, h).start()

    def reduce_second(c):
        zi, j, zz, there = reduce_round(c)
        for h in range(2):
            need(c, h, 1)
            value = partial(place(h, OWN, there, zz), h)
            reduce_cross(c, h).wait_recv()
            value = value + widen(cross_in[c, h])
            if j == 2:
                reduce_ring(zi, h, 0, PAIR).wait_recv()
                value = value + widen(around_in[zi, h, 0])
            if j < 3:
                around[zi, h, j] = narrow(value)
                reduce_ring(zi, h, j, VIA[zi] if j == 0 else there).start()
            else:
                for i in (1, 2):
                    reduce_ring(zi, h, i, PAIR).wait_recv()
                    value = value + widen(around_in[zi, h, i])
                if zi == 0:
                    zs[h] = value.astype(Z_DTYPE)
                    reduce_z(h).start()
                else:
                    grad_t[h] = value

    share = SIDE // PEERS

    def share_of(device):
        return pl.ds(pl.multiple_of(device * share, share), share)

    def psum_one(i):
        peer = (rep + i) % PEERS
        return send(pg.at[share_of(peer)], pr.at[rep], PSUM_ONE + i, peer, "rep")

    def psum_two(i):
        peer = (rep + i) % PEERS
        return send(dl.at[share_of(rep)], dl.at[share_of(rep)], PSUM_TWO + i, peer, "rep")

    def psum_turn(_):
        pr[rep] = pg[share_of(rep)]
        for i in range(1, PEERS):
            psum_one(i).wait_recv()
        dl[share_of(rep)] = jnp.sum(pr[...], axis=0)
        for i in range(1, PEERS):
            psum_two(i).start()

    pl.semaphore_wait(barrier, len(near) + PEERS - 1)
    cot_start(0)
    load_w.wait()
    for h in range(2):
        wg[fsdp, h] = narrow(wf[h * HALF : (h + 1) * HALF])
    gather_step(0)
    load_p.wait()
    for i in range(1, PEERS):
        psum_one(i).start()
    load_c.wait()
    turned = narrow(widen(cb[0]).T)
    ct[0, :, 0:tokens] = turned
    ct[1, :, 0:tokens] = turned
    some = xc.at[pl.ds(0, 16), :, pl.ds(0, tokens)]
    loaded = pltpu.make_async_copy(some, some, load_sem.at[3])

    steps = dict(
        C=cot_start, W=cot_wait, G=gather_step, T=trade_start, P=project, K=keys_start,
        F=reduce_first, S=reduce_second, R=psum_turn, L=lambda _: loaded.wait(),
    )
    for step in PLAN:
        steps[step[0]](int(step[1]))

    for h in range(2):
        reduce_z(h).wait_recv()
        grad_ref[h * HALF : (h + 1) * HALF] = (grad_t[h] + widen(zr[h])).T
    for i in range(1, PEERS):
        peer = (rep + PEERS - i) % PEERS
        send(dl.at[share_of(peer)], dl.at[share_of(peer)], PSUM_TWO + i, peer, "rep").wait_recv()
    delta_ref[...] = dl[...]
    keys_copy(0).wait_recv()
    keys_copy(1).wait_recv()
    proj_ref[...] = narrow(acc[...] + widen(keys_in[0]) + widen(keys_in[1]))

    for i in range(1, PEERS):
        psum_one(i).wait_send()
        psum_two(i).wait_send()
    for h in range(2):
        reduce_z(h).wait_send()
        keys_copy(h).wait_send()
        for part in range(COT_PARTS):
            trade_cot(h, part).wait_send()
        for where in (OWN,) + BY_Z:
            gather_z(h, fsdp, where).wait_send()
        for where in range(RING):
            for r in range(TWO):
                gather_cross(r, h, fsdp, where).wait_send()
                if where != OWN and (r == 0 or where not in BY_Z):
                    gather_ring(r, h, fsdp, where, PAIR).wait_send()
        for zi in range(TWO):
            for j in range(3):
                reduce_ring(zi, h, j, PAIR).wait_send()
        for c in range(COMBOS):
            reduce_cross(c, h).wait_send()
            trade(c, h, 0, OWN).wait_send()
            trade(c, h, 1, OWN).wait_send()


def exchange(tokens, grads_in, master, pseudo):
    n, depth = tokens.shape
    rows, width = master.shape
    bf16, f32 = jnp.bfloat16, jnp.float32
    tall = (width, HALF)
    flops = 4 * n * depth * width
    return pl.pallas_call(
        body,
        out_shape=[
            jax.ShapeDtypeStruct((n, width), bf16),
            jax.ShapeDtypeStruct((rows, width), f32),
            jax.ShapeDtypeStruct(pseudo.shape, f32),
        ],
        in_specs=[pl.BlockSpec(memory_space=pl.ANY)] * 4,
        out_specs=[pl.BlockSpec(memory_space=pltpu.VMEM)] * 3,
        scratch_shapes=[
            pltpu.VMEM((32, 2, 2 * n, HALF), bf16),
            pltpu.VMEM((3, n, width), bf16),
            pltpu.VMEM((2, width, 2 * n), bf16),
            pltpu.VMEM((rows, width), f32),
            pltpu.VMEM((32, 2, HALF, width), bf16),
            pltpu.VMEM((n, width), f32),
            pltpu.VMEM((2, n, width), f32),
            pltpu.VMEM((2, n, width), bf16),
            pltpu.VMEM((2, n, width), bf16),
            pltpu.VMEM((COMBOS, 2) + tall, bf16),
            pltpu.VMEM((COMBOS, 2) + tall, bf16),
            pltpu.VMEM((TWO, 2, 3) + tall, bf16),
            pltpu.VMEM((TWO, 2, 3) + tall, bf16),
            pltpu.VMEM((2,) + tall, Z_DTYPE),
            pltpu.VMEM((2,) + tall, Z_DTYPE),
            pltpu.VMEM((2,) + tall, f32),
            pltpu.VMEM(pseudo.shape, f32),
            pltpu.VMEM((PEERS, SIDE // PEERS, pseudo.shape[1]), f32),
            pltpu.VMEM(pseudo.shape, f32),
            pltpu.SemaphoreType.DMA((4,)),
            pltpu.SemaphoreType.DMA((N_SEMS,)),
            pltpu.SemaphoreType.DMA((N_SEMS,)),
        ],
        compiler_params=pltpu.CompilerParams(
            collective_id=0, has_side_effects=True, vmem_limit_bytes=58 * 2**20
        ),
        cost_estimate=pl.CostEstimate(flops=flops, bytes_accessed=12 * 2**20, transcendentals=0),
    )(tokens, grads_in, master, pseudo)


def finish_body(
    frag_ref, keys_ref, grad_ref, delta_ref, w_ref, one_ref, two_ref, pseudo_ref, anchor_ref, mom_ref,
    keys_out, w_out, one_out, two_out, anchor_out, mom_out,
):
    frag = frag_ref[0]
    keys_out[...] = keys_ref[...]
    frag_w = delta_ref.shape[1]
    mean_delta = delta_ref[...] / PEERS
    pseudo = pseudo_ref[...]
    for q in range(w_ref.shape[1] // frag_w):
        columns = slice(q * frag_w, (q + 1) * frag_w)
        here = frag == q
        momentum, anchor = mom_ref[:, columns], anchor_ref[:, columns]
        new_momentum = outer_momentum * momentum + mean_delta
        update = outer_rate * (outer_momentum * new_momentum + mean_delta)
        mom_out[:, columns] = jnp.where(here, new_momentum, momentum)
        anchor_out[:, columns] = jnp.where(here, anchor - update, anchor)
        master, gradient = w_ref[:, columns], grad_ref[:, columns]
        moment_one = beta_one * one_ref[:, columns] + (1.0 - beta_one) * gradient
        moment_two = beta_two * two_ref[:, columns] + (1.0 - beta_two) * gradient * gradient
        one_out[:, columns] = moment_one
        two_out[:, columns] = moment_two
        stepped = master - inner_rate * (
            moment_one / (jnp.sqrt(moment_two) + adam_epsilon) + weight_decay * master
        )
        w_out[:, columns] = jnp.where(here, stepped + pseudo - update, stepped)


def finish(frag, keys, *states):
    def spec(array):
        rows, columns = array.shape
        return pl.BlockSpec((rows // FINISH_STEPS, columns), lambda i: (i, 0))

    def like(array):
        return jax.ShapeDtypeStruct(array.shape, array.dtype)

    master = states[2]
    outs = [keys] + [master] * 5
    return pl.pallas_call(
        finish_body,
        grid=(FINISH_STEPS,),
        out_shape=[like(out) for out in outs],
        in_specs=[pl.BlockSpec(memory_space=pltpu.SMEM)] + [spec(a) for a in (keys,) + states],
        out_specs=[spec(out) for out in outs],
        cost_estimate=pl.CostEstimate(flops=30 * master.size, bytes_accessed=26 * master.size, transcendentals=2 * master.size),
    )(frag, keys, *states)


def shards(
    inputs, cotangent, weights, first_moment, second_moment, pseudo_grad, anchor, momentum, fragment
):
    keys, gradient, summed = exchange(inputs[0], cotangent[0], weights[0], pseudo_grad[0])
    keys, *states = finish(
        fragment, keys, gradient, summed, weights[0], first_moment[0], second_moment[0],
        pseudo_grad[0], anchor, momentum,
    )
    return keys[None], states[0][None], states[1][None], states[2][None], states[3], states[4]


def solution(mesh):
    return jax.shard_map(
        shards,
        mesh=mesh,
        in_specs=(
            P("rep", "fsdp", None),
            P("rep", "fsdp", None),
            P("rep", "fsdp", None),
            P("rep", "fsdp", None),
            P("rep", "fsdp", None),
            P("rep", "fsdp", None),
            P("fsdp", None),
            P("fsdp", None),
            P(),
        ),
        out_specs=(
            P("rep", "fsdp", None),
            P("rep", "fsdp", None),
            P("rep", "fsdp", None),
            P("rep", "fsdp", None),
            P("fsdp", None),
            P("fsdp", None),
        ),
        check_vma=False,
    )
```

time: 903 us -> 86.1 us (0.10)
  waiting for transfers between devices: 854 us -> 0 us
  Pallas kernels: 0 us -> 84.3 us
  matrix products: 20.4 us -> 0 us
  between operations: 16.3 us -> 1.44 us
    reduce_scatter x1 -> x0, waiting for transfers between devices: 708 us -> none  [shards(): lax.psum_scatter(lax.dot_general(columns, grads_in, (((0,), (0,)), ((), (...]
    all_gather x1 -> x0, waiting for transfers between devices: 145 us -> none  [shards(): lax.all_gather(narrow, 'fsdp', axis=0, tiled=True)]
    pallas_call x0 -> x2, Pallas kernels: none -> 84.3 us  [the longest x1 80.8 us: exchange(): pl.pallas_call(body, out_shape=[jax.ShapeDtypeStruct((n, width), bf16), j...]
    dot_general x2 -> x0, matrix products: 20.4 us -> none  [the longest x1 11.1 us: shards(): lax.dot_general(columns, grads_in, (((0,), (0,)), ((), ())), preferred_el...]
  transfers between devices with their start and end apart: 3 -> 0, of which waited for: 2 -> 0; matrix products, arithmetic and copies ran while one was open for 3% -> 0% of each run, Pallas kernels for 0% -> 0%
where the time goes in v3:
time: 86.1 us; the launch traced here: 85.7 us
  Pallas kernels  84.3 us (98%)
  between operations  1.44 us (2%)
    pallas_call x1, Pallas kernels, exchange(): pl.pallas_call(body, out_shape=[jax.ShapeDtypeStruct((n, width), bf16), j...  80.8 us
    pallas_call x1, Pallas kernels, finish(): pl.pallas_call(finish_body, grid=(FINISH_STEPS,), out_shape=[like(out) fo...  3.43 us

profile of v3, /device:TPU:8, one launch (start us, length us, event | category | flops | bytes accessed | tf_op | source)
XLA Modules:
  0.0 85.7 jit_solution(14624796848977849230)
XLA Ops:
  1.3 80.8 %shard_map.136 = (bf16[384,512]{1,0:T(8,128)(2,1)}, f32[256,512]{1,0:T(8,128)}, f32[256,128]{1,0:T(8,128)}) custom-call(bf16[384,8192]{1,0:T(8,128)(2,1)} %bitcast.16, bf16[384,512]{1,0:T(8,128)(2,1)} %bitcast.20, f32[256,512]{1,0:T(8,128)} %bitcast.10, f32[256,128]{1,0:T(8,128)} %bitcast.14), custom_call_target="tpu_custom_call" | custom-call | flops 6442450944 | bytes 12582912 | tf_op jit(solution)/shard_map/pallas_call | solution.py:326
  82.1 3.4 %shard_map.137 = (bf16[384,512]{1,0:T(8,128)(2,1)}, f32[256,512]{1,0:T(8,128)}, f32[256,512]{1,0:T(8,128)}, f32[256,512]{1,0:T(8,128)}, f32[256,512]{1,0:T(8,128)}, /*index=5*/f32[256,512]{1,0:T(8,128)}) custom-call(s32[1]{0:T(128)S(6)} %copy.15.frag_ref, bf16[384,512]{1,0:T(8,128)(2,1)} %get-tuple-element.15.keys_ref, ...), custom_call_target="tpu_custom_call" | custom-call | flops 3932160 | bytes 3407872 | tf_op jit(solution)/shard_map/pallas_call | solution.py:404

commit v4 on v3

--- a/solution.py
+++ b/solution.py
@@ -26,8 +26,8 @@
 
 OWN, PAIR, FAR, CROSS = range(4)
 GATHER_ORDER = (OWN, CROSS, PAIR, FAR)
-VIA = (CROSS, CROSS)
-BY_Z = (PAIR, FAR)
+VIA = (CROSS, PAIR)
+BY_Z = (FAR,)
 Z_DTYPE = jnp.float32
 
 GATHER_RING = 0
@@ -44,9 +44,9 @@
 N_SEMS = PSUM_TWO + PEERS
 
 PLAN = (
-    "C1", "G1", "T0", "G2", "C2", "G3", "T1", "G4", "T2", "T3", "L0", "W0", "T4", "G5", "F0", "T5",
-    "F1", "S0", "F2", "F3", "P1", "S1", "R0", "P3", "S2", "G6", "T6", "G7", "P4", "F4", "P5", "S3",
-    "T7", "F5", "P2", "F6", "P6", "P0", "P7", "K0", "S4", "S5", "S6", "F7", "S7",
+    "C1", "C2", "T0", "T1", "T2", "T3", "G1", "G2", "T4", "L0", "W0", "F0", "G3", "F1", "S0", "F2",
+    "T5", "S1", "R0", "F3", "S2", "G4", "F4", "F5", "P4", "T6", "S3", "T7", "P5", "G5", "G6", "G7",
+    "P3", "F6", "S4", "P6", "S5", "F7", "P7", "P1", "P2", "P0", "K0", "S6", "D0", "S7",
 )
 
 
@@ -58,7 +58,7 @@
     x_hbm, c_hbm, w_hbm, p_hbm, proj_ref, grad_ref, delta_ref,
     xc, cb, ct, wf, wg, acc, acc_pair, keys, keys_in,
     cross, cross_in, around, around_in,
-    zs, zr, grad_t, pg, pr, dl, load_sem, ss, rs,
+    zs, zr, pg, pr, dl, load_sem, ss, rs,
 ):
     fsdp = lax.axis_index("fsdp")
     rep = lax.axis_index("rep")
@@ -76,6 +76,16 @@
             src_ref=src, dst_ref=dst, send_sem=ss.at[sem], recv_sem=rs.at[sem],
             device_id={axis: device}, device_id_type=MESH,
         )
+
+    flying = []
+
+    def go(copy):
+        copy.start()
+        flying.append(copy)
+
+    def settle(keep):
+        while len(flying) > keep:
+            flying.pop(0).wait_send()
 
     def reduce_round(c):
         zi, j = divmod(c, RING)
@@ -99,20 +109,13 @@
     def block(f, h):
         return x_hbm.at[:, pl.ds(pl.multiple_of(f * SIDE + h * HALF, HALF), HALF)]
 
-    for c in range(COMBOS):
-        _, _, zz, there = reduce_round(c)
-        for h in range(2):
-            for who in (CROSS, OWN):
-                f = place(h, who, there, zz)
-                pltpu.make_async_copy(block(f, h), xc.at[f, h, pl.ds(0, tokens)], load_sem.at[3]).start()
-
     def trade_cot(h, part):
         rows = pl.ds(part * HALF, HALF)
         return send(c_hbm.at[rows], cb.at[1 + h, rows], TRADE_COT + h * COT_PARTS + part, place(h, PAIR, OWN, z))
 
     def cot_start(part):
         for h in range(2):
-            trade_cot(h, part).start()
+            go(trade_cot(h, part))
 
     def cot_wait(_):
         for h in range(2):
@@ -128,8 +131,8 @@
 
     def trade_start(c):
         for h in range(2):
-            trade(c, h, 0, FAR).start()
-            trade(c, h, 1, PAIR).start()
+            go(trade(c, h, 0, FAR))
+            go(trade(c, h, 1, PAIR))
 
     arrived = set()
 
@@ -159,12 +162,12 @@
             if where == OWN:
                 for to in (PAIR, CROSS):
                     if r == 0 or to not in BY_Z:
-                        gather_ring(r, h, f, to, to).start()
-            elif where == CROSS and (r == 0 or FAR not in BY_Z):
-                gather_ring(r, h, f, FAR, PAIR + CROSS - where).start()
+                        go(gather_ring(r, h, f, to, to))
+            elif where == PAIR and (r == 0 or FAR not in BY_Z):
+                go(gather_ring(r, h, f, FAR, PAIR + CROSS - where))
             if r == 0 and (where == OWN or where in BY_Z):
-                gather_z(h, f, where).start()
-            gather_cross(r, h, f, where).start()
+                go(gather_z(h, f, where))
+            go(gather_cross(r, h, f, where))
 
     seen = []
 
@@ -187,7 +190,7 @@
     def keys_start(_):
         for h in range(2):
             keys[h] = narrow(acc_pair[h])
-            keys_copy(h).start()
+            go(keys_copy(h))
 
     def partial(f, h):
         return jnp.dot(ct[h], xc[f, h], preferred_element_type=jnp.float32)
@@ -213,7 +216,7 @@
         for h in range(2):
             need(c, h, 0)
             cross[c, h] = narrow(partial(place(h, CROSS, there, zz), h))
-            reduce_cross(c, h).start()
+            go(reduce_cross(c, h))
 
     def reduce_second(c):
         zi, j, zz, there = reduce_round(c)
@@ -227,16 +230,17 @@
                 value = value + widen(around_in[zi, h, 0])
             if j < 3:
                 around[zi, h, j] = narrow(value)
-                reduce_ring(zi, h, j, VIA[zi] if j == 0 else there).start()
+                go(reduce_ring(zi, h, j, VIA[zi] if j == 0 else there))
             else:
                 for i in (1, 2):
                     reduce_ring(zi, h, i, PAIR).wait_recv()
                     value = value + widen(around_in[zi, h, i])
                 if zi == 0:
                     zs[h] = value.astype(Z_DTYPE)
-                    reduce_z(h).start()
+                    go(reduce_z(h))
                 else:
-                    grad_t[h] = value
+                    reduce_z(h).wait_recv()
+                    grad_ref[h * HALF : (h + 1) * HALF] = (value + widen(zr[h])).T
 
     share = SIDE // PEERS
 
@@ -257,7 +261,14 @@
             psum_one(i).wait_recv()
         dl[share_of(rep)] = jnp.sum(pr[...], axis=0)
         for i in range(1, PEERS):
-            psum_two(i).start()
+            go(psum_two(i))
+
+    def psum_end(_):
+        for i in range(1, PEERS):
+            peer = (rep + PEERS - i) % PEERS
+            send(dl.at[share_of(peer)], dl.at[share_of(peer)], PSUM_TWO + i, peer, "rep").wait_recv()
+        delta_ref[...] = dl[...]
+        settle(24)
 
     pl.semaphore_wait(barrier, len(near) + PEERS - 1)
     cot_start(0)
@@ -265,9 +276,15 @@
     for h in range(2):
         wg[fsdp, h] = narrow(wf[h * HALF : (h + 1) * HALF])
     gather_step(0)
+    for c in range(COMBOS):
+        _, _, zz, there = reduce_round(c)
+        for h in range(2):
+            for who in (CROSS, OWN):
+                f = place(h, who, there, zz)
+                pltpu.make_async_copy(block(f, h), xc.at[f, h, pl.ds(0, tokens)], load_sem.at[3]).start()
     load_p.wait()
     for i in range(1, PEERS):
-        psum_one(i).start()
+        go(psum_one(i))
     load_c.wait()
     turned = narrow(widen(cb[0]).T)
     ct[0, :, 0:tokens] = turned
@@ -277,44 +294,16 @@
 
     steps = dict(
         C=cot_start, W=cot_wait, G=gather_step, T=trade_start, P=project, K=keys_start,
-        F=reduce_first, S=reduce_second, R=psum_turn, L=lambda _: loaded.wait(),
+        F=reduce_first, S=reduce_second, R=psum_turn, D=psum_end, L=lambda _: loaded.wait(),
     )
     for step in PLAN:
         steps[step[0]](int(step[1]))
 
-    for h in range(2):
-        reduce_z(h).wait_recv()
-        grad_ref[h * HALF : (h + 1) * HALF] = (grad_t[h] + widen(zr[h])).T
-    for i in range(1, PEERS):
-        peer = (rep + PEERS - i) % PEERS
-        send(dl.at[share_of(peer)], dl.at[share_of(peer)], PSUM_TWO + i, peer, "rep").wait_recv()
-    delta_ref[...] = dl[...]
     keys_copy(0).wait_recv()
     keys_copy(1).wait_recv()
     proj_ref[...] = narrow(acc[...] + widen(keys_in[0]) + widen(keys_in[1]))
 
-    for i in range(1, PEERS):
-        psum_one(i).wait_send()
-        psum_two(i).wait_send()
-    for h in range(2):
-        reduce_z(h).wait_send()
-        keys_copy(h).wait_send()
-        for part in range(COT_PARTS):
-            trade_cot(h, part).wait_send()
-        for where in (OWN,) + BY_Z:
-            gather_z(h, fsdp, where).wait_send()
-        for where in range(RING):
-            for r in range(TWO):
-                gather_cross(r, h, fsdp, where).wait_send()
-                if where != OWN and (r == 0 or where not in BY_Z):
-                    gather_ring(r, h, fsdp, where, PAIR).wait_send()
-        for zi in range(TWO):
-            for j in range(3):
-                reduce_ring(zi, h, j, PAIR).wait_send()
-        for c in range(COMBOS):
-            reduce_cross(c, h).wait_send()
-            trade(c, h, 0, OWN).wait_send()
-            trade(c, h, 1, OWN).wait_send()
+    settle(0)
 
 
 def exchange(tokens, grads_in, master, pseudo):
@@ -348,7 +337,6 @@
             pltpu.VMEM((TWO, 2, 3) + tall, bf16),
             pltpu.VMEM((2,) + tall, Z_DTYPE),
             pltpu.VMEM((2,) + tall, Z_DTYPE),
-            pltpu.VMEM((2,) + tall, f32),
             pltpu.VMEM(pseudo.shape, f32),
             pltpu.VMEM((PEERS, SIDE // PEERS, pseudo.shape[1]), f32),
             pltpu.VMEM(pseudo.shape, f32),

time: 86.1 us -> 84.1 us (0.977)
  Pallas kernels: 84.3 us -> 82.5 us
    pallas_call x1, Pallas kernels: 80.8 us -> 79.1 us  [exchange(): pl.pallas_call(body, out_shape=[jax.ShapeDtypeStruct((n, width), bf16), j...]
where the time goes in v4:
time: 84.1 us; the launch traced here: 84 us
  Pallas kernels  82.5 us (98%)
  between operations  1.44 us (2%)
    pallas_call x1, Pallas kernels, exchange(): pl.pallas_call(body, out_shape=[jax.ShapeDtypeStruct((n, width), bf16), j...  79.1 us
    pallas_call x1, Pallas kernels, finish(): pl.pallas_call(finish_body, grid=(FINISH_STEPS,), out_shape=[like(out) fo...  3.43 us

profile of v4, /device:TPU:8, one launch (start us, length us, event | category | flops | bytes accessed | tf_op | source)
XLA Modules:
  0.0 84.0 jit_solution(13881794375623679270)
XLA Ops:
  1.3 79.1 %shard_map.136 = (bf16[384,512]{1,0:T(8,128)(2,1)}, f32[256,512]{1,0:T(8,128)}, f32[256,128]{1,0:T(8,128)}) custom-call(bf16[384,8192]{1,0:T(8,128)(2,1)} %bitcast.16, bf16[384,512]{1,0:T(8,128)(2,1)} %bitcast.20, f32[256,512]{1,0:T(8,128)} %bitcast.10, f32[256,128]{1,0:T(8,128)} %bitcast.14), custom_call_target="tpu_custom_call" | custom-call | flops 6442450944 | bytes 12582912 | tf_op jit(solution)/shard_map/pallas_call | solution.py:315
  80.4 3.4 %shard_map.137 = (bf16[384,512]{1,0:T(8,128)(2,1)}, f32[256,512]{1,0:T(8,128)}, f32[256,512]{1,0:T(8,128)}, f32[256,512]{1,0:T(8,128)}, f32[256,512]{1,0:T(8,128)}, /*index=5*/f32[256,512]{1,0:T(8,128)}) custom-call(s32[1]{0:T(128)S(6)} %copy.15.frag_ref, bf16[384,512]{1,0:T(8,128)(2,1)} %get-tuple-element.15.keys_ref, ...), custom_call_target="tpu_custom_call" | custom-call | flops 3932160 | bytes 3407872 | tf_op jit(solution)/shard_map/pallas_call | solution.py:392

commit v5 on v4

--- a/solution.py
+++ b/solution.py
@@ -44,8 +44,8 @@
 N_SEMS = PSUM_TWO + PEERS
 
 PLAN = (
-    "C1", "C2", "T0", "T1", "T2", "T3", "G1", "G2", "T4", "L0", "W0", "F0", "G3", "F1", "S0", "F2",
-    "T5", "S1", "R0", "F3", "S2", "G4", "F4", "F5", "P4", "T6", "S3", "T7", "P5", "G5", "G6", "G7",
+    "C1", "C2", "T0", "T1", "T2", "T3", "G1", "G2", "T4", "L0", "W0", "F0", "G3", "F1", "S0", "R0", "F2",
+    "T5", "S1", "F3", "S2", "G4", "F4", "F5", "P4", "T6", "S3", "T7", "P5", "G5", "G6", "G7",
     "P3", "F6", "S4", "P6", "S5", "F7", "P7", "P1", "P2", "P0", "K0", "S6", "D0", "S7",
 )
 

time: 84.1 us -> 84.1 us (level)
  no operation moved by 1% of the time
where the time goes in v5:
time: 84.1 us; the launch traced here: 84 us
  Pallas kernels  82.5 us (98%)
  between operations  1.44 us (2%)
    pallas_call x1, Pallas kernels, exchange(): pl.pallas_call(body, out_shape=[jax.ShapeDtypeStruct((n, width), bf16), j...  79.1 us
    pallas_call x1, Pallas kernels, finish(): pl.pallas_call(finish_body, grid=(FINISH_STEPS,), out_shape=[like(out) fo...  3.43 us

profile of v5, /device:TPU:8, one launch (start us, length us, event | category | flops | bytes accessed | tf_op | source)
XLA Modules:
  0.0 84.0 jit_solution(16516030245612832091)
XLA Ops:
  1.3 79.1 %shard_map.136 = (bf16[384,512]{1,0:T(8,128)(2,1)}, f32[256,512]{1,0:T(8,128)}, f32[256,128]{1,0:T(8,128)}) custom-call(bf16[384,8192]{1,0:T(8,128)(2,1)} %bitcast.16, bf16[384,512]{1,0:T(8,128)(2,1)} %bitcast.20, f32[256,512]{1,0:T(8,128)} %bitcast.10, f32[256,128]{1,0:T(8,128)} %bitcast.14), custom_call_target="tpu_custom_call" | custom-call | flops 6442450944 | bytes 12582912 | tf_op jit(solution)/shard_map/pallas_call | solution.py:315
  80.4 3.4 %shard_map.137 = (bf16[384,512]{1,0:T(8,128)(2,1)}, f32[256,512]{1,0:T(8,128)}, f32[256,512]{1,0:T(8,128)}, f32[256,512]{1,0:T(8,128)}, f32[256,512]{1,0:T(8,128)}, /*index=5*/f32[256,512]{1,0:T(8,128)}) custom-call(s32[1]{0:T(128)S(6)} %copy.15.frag_ref, bf16[384,512]{1,0:T(8,128)(2,1)} %get-tuple-element.15.keys_ref, ...), custom_call_target="tpu_custom_call" | custom-call | flops 3932160 | bytes 3407872 | tf_op jit(solution)/shard_map/pallas_call | solution.py:392
